TPU v7x, 128 devices: a whole 4x4x4 slice. The times are simulated.
128 devices in a mesh: wide: 32 (over y, z, core), narrow: 4 (over x).
Axes of the slice: x: 4, y: 4, z: 4, core: 2. Of those that a mesh axis runs over, the one named last changes fastest.
Arguments:
- weight: bfloat16 [44544, 14848], P('wide', 'narrow'), may hold values from -36 to 36
- sketch: bfloat16 [14848, 256], P('narrow', 'wide'), may hold values from -4 to 4
Outputs:
- coefficients: bfloat16 [256, 14848], P('wide', 'narrow')
- residual: bfloat16 [44544, 14848], P('wide', 'narrow')
All inputs are finite; a program needn't handle non-finite values.
Results may differ from a plain program's by a relative error of at most 0.0034.
Values may be sent and summed in bfloat16 or wider, within the bound.
A program may use at most 64 MiB of HBM per device.

v0:
```python
import jax
import jax.numpy as jnp
from jax import lax
from jax.sharding import PartitionSpec as P

ITERS = 6


def local_gram(block):
    return jnp.dot(
        block.T, block, precision=lax.Precision.HIGHEST, preferred_element_type=jnp.float32
    )


def shards(weight, sketch):
    partial_image = jnp.dot(
        weight,
        lax.all_gather(sketch, "wide", axis=1, tiled=True),
        preferred_element_type=jnp.float32,
    )
    image = lax.psum(partial_image, "narrow")

    def gram_sum(block):
        return lax.psum(block, "wide")

    total_squares = lax.psum(jnp.sum(image * image), "wide")
    iterate = image / jnp.sqrt(total_squares)
    cross = gram_sum(local_gram(iterate))
    for step in range(ITERS):
        if step > 0:
            cross = gram_sum(local_gram(iterate))
        iterate = 1.5 * iterate - 0.5 * jnp.dot(iterate, cross, precision=lax.Precision.HIGHEST)
    basis = iterate.astype(jnp.bfloat16)
    columns = basis
    coef_own = lax.psum_scatter(
        lax.dot_general(
            columns, weight, (((0,), (0,)), ((), ())), preferred_element_type=jnp.float32
        ),
        "wide",
        scatter_dimension=0,
        tiled=True,
    ).astype(jnp.bfloat16)
    columns = basis
    product = jnp.dot(
        columns,
        lax.all_gather(coef_own, "wide", axis=0, tiled=True),
        preferred_element_type=jnp.float32,
    )
    residual = (weight.astype(jnp.float32) - product).astype(jnp.bfloat16)
    return (coef_own, residual)


def solution(mesh):
    placed = (P("wide", "narrow"), P("narrow", "wide"))
    return jax.shard_map(
        shards,
        mesh=mesh,
        in_specs=placed,
        out_specs=(P("wide", "narrow"), P("wide", "narrow")),
        check_vma=False,
    )
```

profile of v0, /device:TPU:1, one launch (start us, length us, event | category | flops | bytes accessed | tf_op | source)
XLA Modules:
  0.0 1040.0 jit_solution(2418015434875069018)
XLA Ops:
  7.2 0.0 all-gather.3.cloned.1.call-start
  7.2 0.7 all-gather.3.cloned.1.call-update
  7.9 0.0 all-reduce.10.cloned.1.call-start
  7.9 49.8 %all-gather.3.cloned.1.call-done = bf16[3712,256]{0,1:T(8,128)(2,1)} async-done(((bf16[3712,8]{0,1:T(8,128)(2,1)}), bf16[3712,256]{0,1:T(8,128)(2,1)}) %all-gather.3.cloned.1.call-update) | async-done | bytes 1900560 | tf_op jit(solution)/shard_map/all_gather | solution.py:18
  57.8 8.5 fusion.8
  66.3 0.0 all-reduce.10.cloned.1.call-update
  66.3 0.0 all-reduce.12.cloned.1.call-start
  66.4 46.8 %all-reduce.10.cloned.1.call-done = f32[1392,256]{1,0:T(8,128)} async-done(((f32[1392,256]{1,0:T(8,128)}), f32[1392,256]{1,0:T(8,128)}) %all-reduce.10.cloned.1.call-update) | async-done | bytes 1425424 | tf_op jit(solution)/shard_map/psum | solution.py:21
  113.1 2.4 multiply_reduce_fusion
  115.6 64.3 %psum.57 = f32[]{:T(128)} all-reduce(f32[]{:T(128)} %multiply_reduce_fusion), channel_id=1, replica_groups=mesh['wide'=32,'narrow'=4] {'wide'}, use_global_device_ids=true, to_apply=%region_2.0 | all-reduce | flops 1 | bytes 8 | tf_op jit(solution)/shard_map/psum | solution.py:26
  180.6 3.2 fusion.7
  183.8 0.0 all-reduce.12.cloned.1.call-update
  183.8 0.0 all-reduce.14.cloned.1.call-start
  183.9 100.9 %all-reduce.12.cloned.1.call-done = f32[256,256]{1,0:T(8,128)} async-done(((f32[256,256]{1,0:T(8,128)}), f32[256,256]{1,0:T(8,128)}) %all-reduce.12.cloned.1.call-update) | async-done | bytes 262160 | tf_op jit(solution)/shard_map/psum | solution.py:24
  284.8 2.3 fusion.5
  287.0 3.2 fusion.9
  290.2 0.0 all-reduce.14.cloned.1.call-update
  290.2 0.2 all-reduce.16.cloned.1.call-start
  290.5 100.9 %all-reduce.14.cloned.1.call-done = f32[256,256]{1,0:T(8,128)} async-done(((f32[256,256]{1,0:T(8,128)}), f32[256,256]{1,0:T(8,128)}) %all-reduce.14.cloned.1.call-update) | async-done | bytes 262160 | tf_op jit(solution)/shard_map/psum | solution.py:24
  391.4 2.2 fusion.4
  393.6 3.2 fusion.10
  396.8 0.0 all-reduce.16.cloned.1.call-update
  396.8 0.0 all-reduce.18.cloned.1.call-start
  396.9 101.1 %all-reduce.16.cloned.1.call-done = f32[256,256]{1,0:T(8,128)} async-done(((f32[256,256]{1,0:T(8,128)}), f32[256,256]{1,0:T(8,128)}) %all-reduce.16.cloned.1.call-update) | async-done | bytes 262160 | tf_op jit(solution)/shard_map/psum | solution.py:24
  498.0 2.2 fusion.3
  500.2 3.2 fusion.11
  503.4 0.0 all-reduce.18.cloned.1.call-update
  503.5 0.0 all-reduce.20.cloned.1.call-start
  503.5 101.1 %all-reduce.18.cloned.1.call-done = f32[256,256]{1,0:T(8,128)} async-done(((f32[256,256]{1,0:T(8,128)}), f32[256,256]{1,0:T(8,128)}) %all-reduce.18.cloned.1.call-update) | async-done | bytes 262160 | tf_op jit(solution)/shard_map/psum | solution.py:24
  604.6 2.2 fusion.2
  606.9 1.1 copy-done
  608.0 3.2 fusion.12
  611.1 0.0 all-reduce.20.cloned.1.call-update
  611.2 0.3 all-reduce.22.cloned.1.call-start
  611.4 100.9 %all-reduce.20.cloned.1.call-done = f32[256,256]{1,0:T(8,128)} async-done(((f32[256,256]{1,0:T(8,128)}), f32[256,256]{1,0:T(8,128)}) %all-reduce.20.cloned.1.call-update) | async-done | bytes 262160 | tf_op jit(solution)/shard_map/psum | solution.py:24
  712.3 3.2 fusion.1
  715.5 3.2 fusion.13
  718.7 0.0 all-reduce.22.cloned.1.call-update
  718.7 0.0 all-gather.5.cloned.1.call-start
  718.8 0.6 dynamic-slice
  720.0 99.9 %all-reduce.22.cloned.1.call-done = f32[256,256]{1,0:T(8,128)} async-done(((f32[256,256]{1,0:T(8,128)}), f32[256,256]{1,0:T(8,128)}) %all-reduce.22.cloned.1.call-update) | async-done | bytes 262160 | tf_op jit(solution)/shard_map/psum | solution.py:24
  819.9 2.2 fusion.6
  822.1 9.1 fusion.14
  831.2 146.3 %all-reduce.23 = bf16[256,3712]{1,0:T(8,128)(2,1)} all-reduce(f32[256,3712]{1,0:T(8,128)} %fusion.14), channel_id=2, replica_groups=mesh['wide'=32,'narrow'=4] {'wide'}, use_global_device_ids=true, to_apply=%region_9.0.clone | all-reduce | flops 950272 | bytes 5701632
  977.5 1.5 dynamic-slice_convert_fusion
  978.9 0.0 all-gather.5.cloned.1.call-update
  978.9 45.9 %all-gather.5.cloned.1.call-done = bf16[256,3712]{1,0:T(8,128)(2,1)} async-done(((bf16[8,3712]{1,0:T(8,128)(2,1)}), bf16[256,3712]{1,0:T(8,128)(2,1)}) %all-gather.5.cloned.1.call-update) | async-done | bytes 1900560 | tf_op jit(solution)/shard_map/all_gather | solution.py:46
  1024.8 8.7 subtract_convert_fusion
  (5 shorter events, 0.0 us)
Async XLA Ops:
  7.2 50.6 %all-gather.3.cloned.1.call-start = ((), (), s32[]{:S(2)}) async-start(), calls=%async_computation | async-start | bytes 1959936 | tf_op jit(solution)/shard_map/all_gather | solution.py:18
  7.9 105.2 %all-reduce.10.cloned.1.call-start = ((), (), s32[]{:S(2)}) async-start(), calls=%async_computation.1 | async-start | bytes 2850816 | tf_op jit(solution)/shard_map/psum | solution.py:21
  66.3 218.4 %all-reduce.12.cloned.1.call-start = ((), (), s32[]{:S(2)}) async-start(), calls=%async_computation.2 | async-start | bytes 524288 | tf_op jit(solution)/shard_map/psum | solution.py:24
  113.1 67.5 %copy-start.1 = (f32[1392,256]{1,0:T(8,128)S(1)}, f32[1392,256]{1,0:T(8,128)}, u32[]{:S(2)}) copy-start(f32[1392,256]{1,0:T(8,128)} %all-reduce.10.cloned.1.call-done) | copy-start | bytes 4276228
  183.8 207.6 %all-reduce.14.cloned.1.call-start = ((), (), s32[]{:S(2)}) async-start(), calls=%async_computation.3 | async-start | bytes 524288 | tf_op jit(solution)/shard_map/psum | solution.py:24
  290.2 207.8 %all-reduce.16.cloned.1.call-start = ((), (), s32[]{:S(2)}) async-start(), calls=%async_computation.4 | async-start | bytes 524288 | tf_op jit(solution)/shard_map/psum | solution.py:24
  396.8 207.8 %all-reduce.18.cloned.1.call-start = ((), (), s32[]{:S(2)}) async-start(), calls=%async_computation.5 | async-start | bytes 524288 | tf_op jit(solution)/shard_map/psum | solution.py:24
  503.5 208.9 %all-reduce.20.cloned.1.call-start = ((), (), s32[]{:S(2)}) async-start(), calls=%async_computation.6 | async-start | bytes 524288 | tf_op jit(solution)/shard_map/psum | solution.py:24
  606.9 1.1 copy-start
  611.2 208.8 %all-reduce.22.cloned.1.call-start = ((), (), s32[]{:S(2)}) async-start(), calls=%async_computation.7 | async-start | bytes 524288 | tf_op jit(solution)/shard_map/psum | solution.py:24
  715.5 3.3 copy-start.2
  718.7 306.1 %all-gather.5.cloned.1.call-start = ((), (), s32[]{:S(2)}) async-start(), calls=%async_computation.8 | async-start | bytes 1959936 | tf_op jit(solution)/shard_map/all_gather | solution.py:46
Sparse Core Ops, SparseCore 0:
  10.3 47.3 all-gather.2
  66.4 46.6 all-reduce.9
  183.9 100.7 all-reduce.11
  290.4 100.9 all-reduce.13
  397.0 101.0 all-reduce.15
  503.6 100.9 all-reduce.17
  611.3 101.0 all-reduce.19
  718.9 100.9 all-reduce.21
  979.1 45.6 all-gather.4
where the time goes:
time: 1040 us
  waiting for transfers between devices  748 us (72%)
  blocking collectives  211 us (20%)
  matrix products  59.7 us (6%)
  between operations  15.3 us (1%)
    psum x6, waiting for transfers between devices, gram_sum(): return lax.psum(block, 'wide')  605 us
    unnamed x1, blocking collectives  146 us
    psum x1, blocking collectives, shards(): total_squares = lax.psum(jnp.sum(image * image), 'wide')  64.3 us
    all_gather x1, waiting for transfers between devices, shards(): lax.all_gather(sketch, 'wide', axis=1, tiled=True)  49.8 us
    psum x1, waiting for transfers between devices, shards(): image = lax.psum(partial_image, 'narrow')  46.8 us
    all_gather x1, waiting for transfers between devices, shards(): lax.all_gather(coef_own, 'wide', axis=0, tiled=True)  45.9 us
  transfers between devices with their start and end apart: 9, of which 9 were waited for; matrix products, arithmetic and copies ran while one was open for 0% of the time, Pallas kernels for 0%

commit v1 on v0

v1 whole, which is shorter than its diff:
```python
import jax
import jax.numpy as jnp
from jax import lax
from jax.experimental import pallas as pl
from jax.experimental.pallas import tpu as pltpu
from jax.sharding import PartitionSpec as P

ITERS = 6
RING = 4
RANK = 256
ROWS = 1392
COLS = 3712
PAD = 1408
CHUNK = PAD // RING
HALF = CHUNK // 2
BLK = 16
WIDE = 1920
SKIP = COLS - WIDE
PART_A = 1024
PART_B = WIDE - PART_A
MESH = pl.DeviceIdType.MESH
F32 = jnp.float32
BF16 = jnp.bfloat16


def mod4(value):
    return lax.rem(value, RING)


def split(value):
    high = value.astype(BF16)
    return high, (value - high.astype(F32)).astype(BF16)


def dot(a, b):
    return jnp.dot(a, b, preferred_element_type=F32)


def dot_split(a, b):
    a_high, a_low = split(a)
    b_high, b_low = split(b)
    return dot(a_high, b_high) + (dot(a_high, b_low) + dot(a_low, b_high))


def main_kernel(
    w_hbm,
    sk_ref,
    basis_out,
    coef_out,
    w_ref,
    own_sk,
    mate_sk,
    s_ref,
    part_f,
    part_b,
    img_in,
    img_mid,
    x_high,
    x_low,
    gram,
    total,
    gram_pair,
    gram_x,
    gram_y,
    gram_z,
    poly,
    basis,
    basis_t,
    mate_send,
    mate_recv,
    sum_f,
    sum_b,
    rs_in,
    rs_mid,
    row_f,
    row_b,
    col_in_a,
    col_in_b,
    col_mid_a,
    col_mid_b,
    coef,
    local_sem,
    send_sem,
    recv_sem,
):
    wide = lax.axis_index("wide")
    x = lax.axis_index("narrow")
    core = lax.rem(wide, 2)
    chip = wide // 2
    y, z = chip // RING, lax.rem(chip, RING)
    s1, s2 = 1 + 3 * core, 4 - 3 * core
    p1, p2 = z + core * (y - z), y + core * (z - y)
    mate = {"wide": chip * 2 + 1 - core}

    def chip_peer(a1, a2):
        return {"wide": (a1 * s1 + a2 * s2) * 2 + core}

    def y_peer(step):
        return {"wide": (mod4(y + step) * RING + z) * 2 + core}

    def z_peer(step):
        return {"wide": (y * RING + mod4(z + step)) * 2 + core}

    def x_peer(step):
        return {"narrow": mod4(x + step)}

    load_w = pltpu.make_async_copy(w_hbm, w_ref.at[pl.ds(0, ROWS)], local_sem.at[0])
    load_w.start()

    barrier = pltpu.get_barrier_semaphore()
    peers = [mate] + [f(s) for f in (x_peer, y_peer, z_peer) for s in (1, 2, 3)]
    for peer in peers:
        pl.semaphore_signal(barrier, inc=1, device_id=peer, device_id_type=MESH)
    own_sk[...] = sk_ref[...].astype(F32)
    w_ref[pl.ds(ROWS, PAD - ROWS), :] = jnp.zeros((PAD - ROWS, COLS), BF16)
    pl.semaphore_wait(barrier, len(peers))

    count = [0]
    pending = []

    def send(src, dst, peer):
        at = count[0]
        count[0] += 1
        copy = pltpu.make_async_remote_copy(
            src_ref=src,
            dst_ref=dst,
            send_sem=send_sem.at[at],
            recv_sem=recv_sem.at[at],
            device_id=peer,
            device_id_type=MESH,
        )
        copy.start()
        pending.append(copy)
        return copy

    def drain():
        for copy in pending:
            copy.wait_send()
        pending.clear()

    def gather16(buf, off, u, v):
        (pu, su), (pv, sv) = u, v

        def blk(au, av, start=0, width=WIDE):
            rows = pl.ds(pl.multiple_of((au * su + av * sv) * BLK, BLK), BLK)
            return buf.at[rows, pl.ds(pl.multiple_of(off + start, 128), width)]

        def at_u(step):
            return {"wide": (mod4(pu + step) * su + pv * sv) * 2 + core}

        def at_v(step):
            return {"wide": (pu * su + mod4(pv + step) * sv) * 2 + core}

        def both(au):
            block = blk(au, pv)
            return send(block, block, at_v(1)), send(block, block, at_v(3))

        own = blk(pu, pv)
        to_right = send(own, own, at_u(1))
        to_left = send(own, own, at_u(3))
        lines = [both(pu)]
        to_right.wait_recv()
        left = blk(mod4(pu + 3), pv, 0, PART_A)
        opp_a = send(left, left, at_u(1))
        lines.append(both(mod4(pu + 3)))
        to_left.wait_recv()
        right = blk(mod4(pu + 1), pv, PART_A, PART_B)
        opp_b = send(right, right, at_u(3))
        lines.append(both(mod4(pu + 1)))
        order = [pu, mod4(pu + 3), mod4(pu + 1), mod4(pu + 2)]
        last = []

        def forward(j):
            rightward, leftward = lines[j]
            if j % 2 == 0:
                rightward.wait_recv()
                block = blk(order[j], mod4(pv + 3))
                last.append(send(block, block, at_v(1)))
                last.append(leftward)
            else:
                leftward.wait_recv()
                block = blk(order[j], mod4(pv + 1))
                last.append(send(block, block, at_v(3)))
                last.append(rightward)

        forward(0)
        opp_a.wait_recv()
        opp_b.wait_recv()
        lines.append(both(mod4(pu + 2)))
        forward(1)
        forward(2)
        forward(3)
        for copy in last:
            copy.wait_recv()
        drain()

    axis1, axis2 = (p1, s1), (p2, s2)
    my_off = core * SKIP
    only_off = core * WIDE
    mate_off = (1 - core) * SKIP

    my_cols = pl.ds(pl.multiple_of(my_off, 128), WIDE)
    first = send(own_sk.at[:, pl.ds(pl.multiple_of(mate_off, 128), WIDE)], mate_sk, mate)
    first.wait_recv()
    mine, other = own_sk[:, my_cols], mate_sk[...]
    even = core == 0
    pair = jnp.concatenate([jnp.where(even, mine, other), jnp.where(even, other, mine)], axis=0)
    s_ref[pl.ds(pl.multiple_of(chip * BLK, BLK), BLK), my_cols] = pair.astype(BF16)
    gather16(s_ref, my_off, axis1, axis2)
    half = s_ref.at[:, pl.ds(pl.multiple_of(only_off, 128), SKIP)]
    swap = send(half, half, mate)
    load_w.wait()
    swap.wait_recv()
    drain()

    def chunk_rows(step):
        return pl.multiple_of(mod4(x + step) * CHUNK, 16)

    def image_chunk(step):
        start = chunk_rows(step)
        value = lax.dot_general(
            w_ref[pl.ds(start, CHUNK), :],
            s_ref[...],
            (((1,), (1,)), ((), ())),
            preferred_element_type=F32,
        )
        part_f[pl.ds(start, CHUNK), :] = value
        part_b[pl.ds(start, CHUNK), :] = value.astype(BF16)

    def half_rows(step, second):
        return pl.ds(pl.multiple_of(chunk_rows(step) + second * HALF, 16), HALF)

    image_chunk(2)
    in0 = send(part_b.at[half_rows(2, 0)], img_in.at[0], x_peer(1))
    in1 = send(part_b.at[half_rows(2, 1)], img_in.at[1], x_peer(3))
    image_chunk(1)
    in2 = send(part_b.at[half_rows(1, 1)], img_in.at[2], x_peer(1))
    image_chunk(3)
    in3 = send(part_b.at[half_rows(3, 0)], img_in.at[3], x_peer(3))
    in0.wait_recv()
    img_mid[0] = (part_f[half_rows(1, 0), :] + img_in[0].astype(F32)).astype(BF16)
    in4 = send(img_mid.at[0], img_in.at[4], x_peer(1))
    in1.wait_recv()
    img_mid[1] = (part_f[half_rows(3, 1), :] + img_in[1].astype(F32)).astype(BF16)
    in5 = send(img_mid.at[1], img_in.at[5], x_peer(3))
    image_chunk(0)
    in3.wait_recv()
    in2.wait_recv()
    in4.wait_recv()
    half_a = part_f[half_rows(0, 0), :] + img_in[3].astype(F32) + img_in[4].astype(F32)
    in5.wait_recv()
    half_b = part_f[half_rows(0, 1), :] + img_in[2].astype(F32) + img_in[5].astype(F32)
    own_high, own_low = split(jnp.concatenate([half_a, half_b], axis=0))
    x_high[pl.ds(chunk_rows(0), CHUNK), :] = own_high
    x_low[pl.ds(chunk_rows(0), CHUNK), :] = own_low
    drain()

    def gram_dot(a, b):
        return lax.dot_general(a, b, (((0,), (0,)), ((), ())), preferred_element_type=F32)

    gram[...] = gram_dot(own_high, own_high) + (
        gram_dot(own_high, own_low) + gram_dot(own_low, own_high)
    )
    g_core = pl.multiple_of(core * 128, 128)
    g_mate = pl.multiple_of((1 - core) * 128, 128)
    copy = send(gram.at[pl.ds(g_mate, 128)], gram_pair, mate)
    copy.wait_recv()
    gram[pl.ds(g_core, 128), :] = gram[pl.ds(g_core, 128), :] + gram_pair[...]

    def gram_rows(ax, ay, rows):
        return pl.ds(pl.multiple_of(core * 128 + ax * 32 + ay * 8, 8), rows)

    copies = [
        send(gram.at[gram_rows(mod4(x + s), 0, 32)], gram_x.at[s - 1], x_peer(s)) for s in (1, 2, 3)
    ]
    for copy in copies:
        copy.wait_recv()
    at_x = gram_rows(x, 0, 32)
    gram[at_x, :] = gram[at_x, :] + gram_x[0] + gram_x[1] + gram_x[2]

    def gather_x(buf):
        mine = buf.at[pl.ds(chunk_rows(0), CHUNK)]
        rightward = send(mine, mine, x_peer(1))
        leftward = send(mine, mine, x_peer(3))

        def middle():
            rightward.wait_recv()
            piece = buf.at[half_rows(3, 0)]
            a = send(piece, piece, x_peer(1))
            leftward.wait_recv()
            piece = buf.at[half_rows(1, 1)]
            b = send(piece, piece, x_peer(3))

            def end():
                a.wait_recv()
                b.wait_recv()

            return end

        return middle

    high_middle = gather_x(x_high)
    copies = [
        send(gram.at[gram_rows(x, mod4(y + s), 8)], gram_y.at[s - 1], y_peer(s)) for s in (1, 2, 3)
    ]
    for copy in copies:
        copy.wait_recv()
    at_y = gram_rows(x, y, 8)
    gram[at_y, :] = gram[at_y, :] + gram_y[0] + gram_y[1] + gram_y[2]
    copies = [send(gram.at[at_y], gram_z.at[s - 1], z_peer(s)) for s in (1, 2, 3)]
    for copy in copies:
        copy.wait_recv()
    total[at_y, :] = gram[at_y, :] + gram_z[0] + gram_z[1] + gram_z[2]
    copies = [send(total.at[at_y], total.at[at_y], y_peer(s)) for s in (1, 2, 3)]
    high_end = high_middle()
    for copy in copies:
        copy.wait_recv()
    copies = [send(total.at[at_x], total.at[at_x], x_peer(s)) for s in (1, 2, 3)]
    for copy in copies:
        copy.wait_recv()
    rows = pl.ds(g_core, 128)
    copy = send(total.at[rows], total.at[rows], mate)
    low_middle = gather_x(x_low)
    copy.wait_recv()

    whole = total[...]
    diagonal = lax.broadcasted_iota(jnp.int32, (RANK, RANK), 0) == lax.broadcasted_iota(
        jnp.int32, (RANK, RANK), 1
    )
    trace = jnp.sum(jnp.where(diagonal, whole, 0.0), keepdims=True)
    poly[pl.ds(0, RANK), :] = whole / trace
    poly[pl.ds(RANK, RANK), :] = jnp.where(diagonal, 1.0 / jnp.sqrt(trace), 0.0)

    def factor(g):
        return jnp.where(diagonal, 1.5, 0.0) - 0.5 * g

    def iteration(_, carry):
        both = poly[...]
        p = factor(both[:RANK])
        p_high, p_low = split(p)

        def times_p(a):
            a_high, a_low = split(a)
            return dot(a_high, p_high) + (dot(a_high, p_low) + dot(a_low, p_high))

        both = times_p(both)
        poly[pl.ds(RANK, RANK), :] = both[RANK:]
        poly[pl.ds(0, RANK), :] = times_p(both[:RANK])
        return carry

    lax.fori_loop(0, ITERS - 1, iteration, 0)
    low_end = low_middle()
    high_end()
    q = dot_split(poly[pl.ds(RANK, RANK), :], factor(poly[pl.ds(0, RANK), :]))
    q_high, q_low = split(q)
    low_end()

    basis[...] = (
        dot(x_high[...], q_high) + (dot(x_high[...], q_low) + dot(x_low[...], q_high))
    ).astype(BF16)
    save_basis = pltpu.make_async_copy(basis.at[pl.ds(0, ROWS)], basis_out, local_sem.at[1])
    save_basis.start()
    basis_t[...] = basis[...].T

    def partial(off, start, width):
        cols = pl.ds(pl.multiple_of(off + start, 128), width)
        return dot(basis_t[...], w_ref[:, cols])

    def cols(part):
        return pl.ds(0, PART_A) if part == 0 else pl.ds(PART_A, PART_B)

    copies = []
    for part, (start, width) in enumerate(((0, PART_A), (PART_A, PART_B))):
        mate_send[:, cols(part)] = partial(mate_off, start, width).astype(BF16)
        copies.append(send(mate_send.at[:, cols(part)], mate_recv.at[:, cols(part)], mate))
    for part, (start, width) in enumerate(((0, PART_A), (PART_A, PART_B))):
        value = partial(my_off, start, width)
        copies[part].wait_recv()
        value = value + mate_recv[:, cols(part)].astype(F32)
        sum_f[:, cols(part)] = value
        sum_b[:, cols(part)] = value.astype(BF16)

    def rows_of(a1, a2):
        return pl.ds(pl.multiple_of((a1 * s1 + a2 * s2) * BLK, BLK), BLK)

    u1, u2, u3 = mod4(p1 + 1), mod4(p1 + 2), mod4(p1 + 3)
    right1, left1 = chip_peer(u1, p2), chip_peer(u3, p2)
    in0 = [send(sum_b.at[rows_of(u2, v)], rs_in.at[0, v], right1) for v in (0, 1)]
    in1 = [send(sum_b.at[rows_of(u2, v + 2)], rs_in.at[1, v], left1) for v in (0, 1)]
    in2 = [send(sum_b.at[rows_of(u1, v + 2)], rs_in.at[2, v], right1) for v in (0, 1)]
    in3 = [send(sum_b.at[rows_of(u3, v)], rs_in.at[3, v], left1) for v in (0, 1)]
    in4, in5 = [], []
    for v in (0, 1):
        in0[v].wait_recv()
        rs_mid[0, v] = (sum_f[rows_of(u1, v), :] + rs_in[0, v].astype(F32)).astype(BF16)
        in4.append(send(rs_mid.at[0, v], rs_in.at[4, v], right1))
        in1[v].wait_recv()
        rs_mid[1, v] = (sum_f[rows_of(u3, v + 2), :] + rs_in[1, v].astype(F32)).astype(BF16)
        in5.append(send(rs_mid.at[1, v], rs_in.at[5, v], left1))
    for v in (0, 1):
        in3[v].wait_recv()
        in4[v].wait_recv()
        value = sum_f[rows_of(p1, v), :] + rs_in[3, v].astype(F32) + rs_in[4, v].astype(F32)
        row_f[v] = value
        row_b[v] = value.astype(BF16)
        in2[v].wait_recv()
        in5[v].wait_recv()
        value = sum_f[rows_of(p1, v + 2), :] + rs_in[2, v].astype(F32) + rs_in[5, v].astype(F32)
        row_f[v + 2] = value
        row_b[v + 2] = value.astype(BF16)

    v1, v2, v3 = mod4(p2 + 1), mod4(p2 + 2), mod4(p2 + 3)
    right2, left2 = chip_peer(p1, v1), chip_peer(p1, v3)
    ca, cb = cols(0), cols(1)
    in0 = send(row_b.at[v2, :, ca], col_in_a.at[0], right2)
    in1 = send(row_b.at[v2, :, cb], col_in_b.at[0], left2)
    in2 = send(row_b.at[v1, :, cb], col_in_b.at[1], right2)
    in3 = send(row_b.at[v3, :, ca], col_in_a.at[1], left2)
    in0.wait_recv()
    col_mid_a[...] = (row_f[v1, :, ca] + col_in_a[0].astype(F32)).astype(BF16)
    in4 = send(col_mid_a, col_in_a.at[2], right2)
    in1.wait_recv()
    col_mid_b[...] = (row_f[v3, :, cb] + col_in_b[0].astype(F32)).astype(BF16)
    in5 = send(col_mid_b, col_in_b.at[2], left2)
    in3.wait_recv()
    in4.wait_recv()
    my_rows = pl.ds(pl.multiple_of(chip * BLK, BLK), BLK)
    coef[my_rows, pl.ds(pl.multiple_of(my_off, 128), PART_A)] = (
        row_f[p2, :, ca] + col_in_a[1].astype(F32) + col_in_a[2].astype(F32)
    ).astype(BF16)
    in2.wait_recv()
    in5.wait_recv()
    coef[my_rows, pl.ds(pl.multiple_of(my_off + PART_A, 128), PART_B)] = (
        row_f[p2, :, cb] + col_in_b[1].astype(F32) + col_in_b[2].astype(F32)
    ).astype(BF16)
    drain()

    gather16(coef, my_off, axis2, axis1)
    half = coef.at[:, pl.ds(pl.multiple_of(only_off, 128), SKIP)]
    swap = send(half, half, mate)
    swap.wait_recv()
    drain()
    save_coef = pltpu.make_async_copy(coef, coef_out, local_sem.at[2])
    save_coef.start()
    save_basis.wait()
    save_coef.wait()
    assert count[0] <= COPIES, count[0]


COPIES = 128


def residual_kernel(w_ref, basis_ref, coef_ref, residual_ref, own_ref):
    @pl.when(pl.program_id(0) == 0)
    def _():
        wide = lax.axis_index("wide")
        block = coef_ref[pl.ds(pl.multiple_of((wide // 2) * BLK, BLK), BLK), :].astype(F32)
        first = lax.rem(wide, 2) == 0
        own_ref[...] = jnp.where(first, block[:8], block[8:]).astype(BF16)

    product = dot(basis_ref[...], coef_ref[...])
    residual_ref[...] = (w_ref[...].astype(F32) - product).astype(BF16)


def shards(weight, sketch):
    basis, coef = pl.pallas_call(
        main_kernel,
        out_shape=(
            jax.ShapeDtypeStruct((ROWS, RANK), BF16),
            jax.ShapeDtypeStruct((RANK, COLS), BF16),
        ),
        in_specs=[pl.BlockSpec(memory_space=pl.ANY), pl.BlockSpec(memory_space=pltpu.VMEM)],
        out_specs=[pl.BlockSpec(memory_space=pl.ANY)] * 2,
        scratch_shapes=[
            pltpu.VMEM((PAD, COLS), BF16),
            pltpu.VMEM((8, COLS), F32),
            pltpu.VMEM((8, WIDE), F32),
            pltpu.VMEM((RANK, COLS), BF16),
            pltpu.VMEM((PAD, RANK), F32),
            pltpu.VMEM((PAD, RANK), BF16),
            pltpu.VMEM((6, HALF, RANK), BF16),
            pltpu.VMEM((2, HALF, RANK), BF16),
            pltpu.VMEM((PAD, RANK), BF16),
            pltpu.VMEM((PAD, RANK), BF16),
            pltpu.VMEM((RANK, RANK), F32),
            pltpu.VMEM((RANK, RANK), F32),
            pltpu.VMEM((128, RANK), F32),
            pltpu.VMEM((3, 32, RANK), F32),
            pltpu.VMEM((3, 8, RANK), F32),
            pltpu.VMEM((3, 8, RANK), F32),
            pltpu.VMEM((2 * RANK, RANK), F32),
            pltpu.VMEM((PAD, RANK), BF16),
            pltpu.VMEM((RANK, PAD), BF16),
            pltpu.VMEM((RANK, WIDE), BF16),
            pltpu.VMEM((RANK, WIDE), BF16),
            pltpu.VMEM((RANK, WIDE), F32),
            pltpu.VMEM((RANK, WIDE), BF16),
            pltpu.VMEM((6, 2, BLK, WIDE), BF16),
            pltpu.VMEM((2, 2, BLK, WIDE), BF16),
            pltpu.VMEM((4, BLK, WIDE), F32),
            pltpu.VMEM((4, BLK, WIDE), BF16),
            pltpu.VMEM((3, BLK, PART_A), BF16),
            pltpu.VMEM((3, BLK, PART_B), BF16),
            pltpu.VMEM((BLK, PART_A), BF16),
            pltpu.VMEM((BLK, PART_B), BF16),
            pltpu.VMEM((RANK, COLS), BF16),
            pltpu.SemaphoreType.DMA((3,)),
            pltpu.SemaphoreType.DMA((COPIES,)),
            pltpu.SemaphoreType.DMA((COPIES,)),
        ],
        compiler_params=pltpu.CompilerParams(
            collective_id=0, has_side_effects=True, vmem_limit_bytes=44 * 1024 * 1024
        ),
        cost_estimate=pl.CostEstimate(
            flops=2 * 2 * ROWS * COLS * RANK, bytes_accessed=2 * ROWS * COLS, transcendentals=0
        ),
        name="polar_basis",
    )(weight, sketch.T)

    rows = 240
    residual, own = pl.pallas_call(
        residual_kernel,
        grid=(pl.cdiv(ROWS, rows),),
        out_shape=(
            jax.ShapeDtypeStruct((ROWS, COLS), BF16),
            jax.ShapeDtypeStruct((8, COLS), BF16),
        ),
        in_specs=[
            pl.BlockSpec((rows, COLS), lambda i: (i, 0)),
            pl.BlockSpec((rows, RANK), lambda i: (i, 0)),
            pl.BlockSpec((RANK, COLS), lambda i: (0, 0)),
        ],
        out_specs=[
            pl.BlockSpec((rows, COLS), lambda i: (i, 0)),
            pl.BlockSpec((8, COLS), lambda i: (0, 0)),
        ],
        compiler_params=pltpu.CompilerParams(vmem_limit_bytes=24 * 1024 * 1024),
        cost_estimate=pl.CostEstimate(
            flops=2 * ROWS * COLS * RANK, bytes_accessed=4 * ROWS * COLS, transcendentals=0
        ),
        name="residual",
    )(weight, basis, coef)
    return own, residual


def solution(mesh):
    placed = (P("wide", "narrow"), P("narrow", "wide"))
    return jax.shard_map(
        shards,
        mesh=mesh,
        in_specs=placed,
        out_specs=(P("wide", "narrow"), P("wide", "narrow")),
        check_vma=False,
    )
```

time: 1040 us -> 113 us (0.11)
  waiting for transfers between devices: 748 us -> 0 us
  blocking collectives: 211 us -> 0 us
  Pallas kernels: 0 us -> 111 us
  matrix products: 59.7 us -> 0 us
  between operations: 15.3 us -> 0.69 us
    psum x7 -> x0, waiting for transfers between devices: 652 us -> none  [the longest x6 605 us: gram_sum(): return lax.psum(block, 'wide')]
    unnamed x1 -> x0, blocking collectives: 146 us -> none
    pallas_call x0 -> x2, Pallas kernels: none -> 111 us  [the longest x1 104 us: shards(): pl.pallas_call(main_kernel, out_shape=(jax.ShapeDtypeStruct((ROWS, RANK),...]
    all_gather x2 -> x0, waiting for transfers between devices: 95.7 us -> none  [the longest x1 49.8 us: shards(): lax.all_gather(sketch, 'wide', axis=1, tiled=True)]
    psum x1 -> x0, blocking collectives: 64.3 us -> none  [shards(): total_squares = lax.psum(jnp.sum(image * image), 'wide')]
    dot_general x15 -> x0, matrix products: 59.7 us -> none  [the longest x6 19.1 us: local_gram(): jnp.dot(block.T, block, precision=lax.Precision.HIGHEST, preferred_elemen...]
  transfers between devices with their start and end apart: 9 -> 0, of which waited for: 9 -> 0; matrix products, arithmetic and copies ran while one was open for 0% -> 0% of each run, Pallas kernels for 0% -> 0%
where the time goes in v1:
time: 113 us; the launch traced here: 112 us
  Pallas kernels  111 us (98%)
    pallas_call x1, Pallas kernels, shards(): pl.pallas_call(main_kernel, out_shape=(jax.ShapeDtypeStruct((ROWS, RANK),...  104 us
    pallas_call x1, Pallas kernels, shards(): pl.pallas_call(residual_kernel, grid=(pl.cdiv(ROWS, rows),), out_shape=(j...  6.38 us

profile of v1, /device:TPU:1, one launch (start us, length us, event | category | flops | bytes accessed | tf_op | source)
XLA Modules:
  0.0 112.5 jit_solution(4767032976287330453)
XLA Ops:
  0.6 0.0 slice-start
  0.6 0.0 copy-start
  0.6 1.0 copy-done
  1.6 0.0 slice-start.1
  1.6 0.0 slice-start.2
  1.6 104.4 %polar_basis.1 = (bf16[1392,256]{1,0:T(8,128)(2,1)S(1)}, bf16[256,3712]{1,0:T(8,128)(2,1)S(1)}) custom-call(bf16[1392,3712]{1,0:T(8,128)(2,1)} %w_ref.1, bf16[8,3712]{1,0:T(8,128)(2,1)S(1)} %bitcast.3), custom_call_target="tpu_custom_call" | custom-call | flops 5291114496 | bytes 10334208 | tf_op jit(solution)/shard_map/polar_basis/pallas_call | solution.py:466
  106.1 0.0 slice-done
  106.1 0.0 slice-done.1
  106.1 0.0 slice-done.2
  106.1 6.4 %residual.1 = (bf16[1392,3712]{1,0:T(8,128)(2,1)}, bf16[8,3712]{1,0:T(8,128)(2,1)}) custom-call(bf16[1392,3712]{1,0:T(8,128)(2,1)S(1)} %bitcast.2, bf16[1392,256]{1,0:T(8,128)(2,1)S(1)} %get-tuple-element.6.basis_ref, bf16[256,3712]{1,0:T(8,128)(2,1)S(1)} %get-tuple-element.7.coef_ref), custom_call_target="tpu_custom_call" | custom-call | flops 2645557248 | bytes 20668416 | tf_op jit(solution)/shard_map/residual/pallas_call | solution.py:521
  (1 shorter events, 0.0 us)
Async XLA Ops:
  0.6 105.4 %slice-start = ((s8[10334208]{0:T(1024)(128)(4,1)}), s8[4194304]{0:T(1024)(128)(4,1)S(1)}, s32[]{:S(2)}) async-start(s8[10334208]{0:T(1024)(128)(4,1)} %bitcast.1), calls=%async_computation | async-start | bytes 8388608
  0.6 1.0 copy-start
  1.6 104.5 %slice-start.1 = ((s8[10334208]{0:T(1024)(128)(4,1)}), s8[4194304]{0:T(1024)(128)(4,1)S(1)}, s32[]{:S(2)}) async-start(s8[10334208]{0:T(1024)(128)(4,1)} %bitcast.1), calls=%async_computation.1 | async-start | bytes 8388608
  1.6 104.5 %slice-start.2 = ((s8[10334208]{0:T(1024)(128)(4,1)}), s8[1945600]{0:T(1024)(128)(4,1)S(1)}, s32[]{:S(2)}) async-start(s8[10334208]{0:T(1024)(128)(4,1)} %bitcast.1), calls=%async_computation.2 | async-start | bytes 3891200

commit v2 on v1

v2 whole, which is shorter than its diff:
```python
import jax
import jax.numpy as jnp
from jax import lax
from jax.experimental import pallas as pl
from jax.experimental.pallas import tpu as pltpu
from jax.sharding import PartitionSpec as P

ITERS = 6
RING = 4
RANK = 256
ROWS = 1392
COLS = 3712
PAD = 1408
CHUNK = PAD // RING
HALF = CHUNK // 2
BLK = 16
WIDE = 1920
SKIP = COLS - WIDE
TILES = 16
SKIP2 = COLS - TILES * 128
PART = TILES * 64
MESH = pl.DeviceIdType.MESH
F32 = jnp.float32
BF16 = jnp.bfloat16


def mod4(value):
    return lax.rem(value, RING)


def split(value):
    high = value.astype(BF16)
    return high, (value - high.astype(F32)).astype(BF16)


def dot(a, b):
    return jnp.dot(a, b, preferred_element_type=F32)


def dot_split(a, b):
    a_high, a_low = split(a)
    b_high, b_low = split(b)
    return dot(a_high, b_high) + (dot(a_high, b_low) + dot(a_low, b_high))


def main_kernel(
    w_hbm,
    sk_ref,
    basis_out,
    coef_out,
    w_ref,
    own_sk,
    mate_sk,
    s_ref,
    part_f,
    part_b,
    img_in,
    img_mid,
    gram,
    total,
    gram_pair,
    gram_x,
    gram_y,
    gram_z,
    poly,
    basis,
    img,
    img_t,
    mate_send,
    mate_recv,
    z_f,
    z_b,
    z_in,
    row_f,
    row_b,
    col_in,
    coef,
    coef_mate,
    local_sem,
    send_sem,
    recv_sem,
):
    wide = lax.axis_index("wide")
    x = lax.axis_index("narrow")
    core = lax.rem(wide, 2)
    chip = wide // 2
    y, z = chip // RING, lax.rem(chip, RING)
    s1, s2 = 1 + 3 * core, 4 - 3 * core
    p1, p2 = z + core * (y - z), y + core * (z - y)
    mate = {"wide": chip * 2 + 1 - core}

    def chip_peer(a1, a2):
        return {"wide": (a1 * s1 + a2 * s2) * 2 + core}

    def y_peer(step):
        return {"wide": (mod4(y + step) * RING + z) * 2 + core}

    def z_peer(step):
        return {"wide": (y * RING + mod4(z + step)) * 2 + core}

    def x_peer(step):
        return {"narrow": mod4(x + step)}

    load_w = pltpu.make_async_copy(w_hbm, w_ref.at[pl.ds(0, ROWS)], local_sem.at[0])
    load_w.start()

    barrier = pltpu.get_barrier_semaphore()
    peers = [mate] + [f(s) for f in (x_peer, y_peer, z_peer) for s in (1, 2, 3)]
    for peer in peers:
        pl.semaphore_signal(barrier, inc=1, device_id=peer, device_id_type=MESH)
    own_sk[...] = sk_ref[...].astype(F32)
    w_ref[pl.ds(ROWS, PAD - ROWS), :] = jnp.zeros((PAD - ROWS, COLS), BF16)
    pl.semaphore_wait(barrier, len(peers))

    count = [0]
    pending = []

    def send(src, dst, peer):
        at = count[0]
        count[0] += 1
        copy = pltpu.make_async_remote_copy(
            src_ref=src,
            dst_ref=dst,
            send_sem=send_sem.at[at],
            recv_sem=recv_sem.at[at],
            device_id=peer,
            device_id_type=MESH,
        )
        copy.start()
        pending.append(copy)
        return copy

    def drain():
        for copy in pending:
            copy.wait_send()
        pending.clear()

    def gather16(blk, u, v, share):
        (pu, su), (pv, sv) = u, v

        def at_u(step):
            return {"wide": (mod4(pu + step) * su + pv * sv) * 2 + core}

        def at_v(step):
            return {"wide": (pu * su + mod4(pv + step) * sv) * 2 + core}

        own = blk(pu, pv)
        along_u = {s: send(own, own, at_u(s)) for s in (2, 1, 3)}
        along_v = [(pu, {s: send(own, own, at_v(s)) for s in (2, 1, 3)})]
        shared = [share(pu, pv)]
        for s in (1, 3, 2):
            along_u[s].wait_recv()
            a = mod4(pu + 4 - s)
            block = blk(a, pv)
            along_v.append((a, {t: send(block, block, at_v(t)) for t in (2, 1, 3)}))
            shared.append(share(a, pv))
        for a, copies in along_v:
            for t in (1, 3, 2):
                copies[t].wait_recv()
                shared.append(share(a, mod4(pv + 4 - t)))
        for copy in shared:
            copy.wait_recv()
        drain()

    axis1, axis2 = (p1, s1), (p2, s2)
    my_off = core * SKIP
    only_off = core * WIDE
    mate_off = (1 - core) * SKIP
    my_off2, mate_off2 = core * SKIP2, (1 - core) * SKIP2

    my_cols = pl.ds(pl.multiple_of(my_off, 128), WIDE)
    first = send(own_sk.at[:, pl.ds(pl.multiple_of(mate_off, 128), WIDE)], mate_sk, mate)
    first.wait_recv()
    mine, other = own_sk[:, my_cols], mate_sk[...]
    even = core == 0
    pair = jnp.concatenate([jnp.where(even, mine, other), jnp.where(even, other, mine)], axis=0)
    s_ref[pl.ds(pl.multiple_of(chip * BLK, BLK), BLK), my_cols] = pair.astype(BF16)

    def sketch_block(a1, a2):
        return s_ref.at[pl.ds(pl.multiple_of((a1 * s1 + a2 * s2) * BLK, BLK), BLK), my_cols]

    def share_sketch(a1, a2):
        rows = pl.ds(pl.multiple_of((a1 * s1 + a2 * s2) * BLK, BLK), BLK)
        block = s_ref.at[rows, pl.ds(pl.multiple_of(only_off, 128), SKIP)]
        return send(block, block, mate)

    gather16(sketch_block, axis1, axis2, share_sketch)
    load_w.wait()

    def chunk_rows(step):
        return pl.multiple_of(mod4(x + step) * CHUNK, 16)

    def image_chunk(step):
        start = chunk_rows(step)
        value = lax.dot_general(
            w_ref[pl.ds(start, CHUNK), :],
            s_ref[...],
            (((1,), (1,)), ((), ())),
            preferred_element_type=F32,
        )
        part_f[pl.ds(start, CHUNK), :] = value
        part_b[pl.ds(start, CHUNK), :] = value.astype(BF16)

    def half_rows(step, second):
        return pl.ds(pl.multiple_of(chunk_rows(step) + second * HALF, 16), HALF)

    image_chunk(2)
    in0 = send(part_b.at[half_rows(2, 0)], img_in.at[0], x_peer(1))
    in1 = send(part_b.at[half_rows(2, 1)], img_in.at[1], x_peer(3))
    image_chunk(1)
    in2 = send(part_b.at[half_rows(1, 1)], img_in.at[2], x_peer(1))
    image_chunk(3)
    in3 = send(part_b.at[half_rows(3, 0)], img_in.at[3], x_peer(3))
    in0.wait_recv()
    img_mid[0] = (part_f[half_rows(1, 0), :] + img_in[0].astype(F32)).astype(BF16)
    in4 = send(img_mid.at[0], img_in.at[4], x_peer(1))
    in1.wait_recv()
    img_mid[1] = (part_f[half_rows(3, 1), :] + img_in[1].astype(F32)).astype(BF16)
    in5 = send(img_mid.at[1], img_in.at[5], x_peer(3))
    image_chunk(0)
    in3.wait_recv()
    in4.wait_recv()
    own_a, own_b = half_rows(0, 0), half_rows(0, 1)
    img[own_a, :] = (part_f[own_a, :] + img_in[3].astype(F32) + img_in[4].astype(F32)).astype(BF16)
    a_right = send(img.at[own_a], img.at[own_a], x_peer(1))
    in2.wait_recv()
    in5.wait_recv()
    img[own_b, :] = (part_f[own_b, :] + img_in[2].astype(F32) + img_in[5].astype(F32)).astype(BF16)
    b_left = send(img.at[own_b], img.at[own_b], x_peer(3))
    b_right = send(img.at[own_b], img.at[own_b], x_peer(1))
    a_left = send(img.at[own_a], img.at[own_a], x_peer(3))

    own = img[pl.ds(chunk_rows(0), CHUNK), :]
    gram[...] = lax.dot_general(own, own, (((0,), (0,)), ((), ())), preferred_element_type=F32)
    g_core = pl.multiple_of(core * 128, 128)
    g_mate = pl.multiple_of((1 - core) * 128, 128)
    copy = send(gram.at[pl.ds(g_mate, 128)], gram_pair, mate)
    copy.wait_recv()
    gram[pl.ds(g_core, 128), :] = gram[pl.ds(g_core, 128), :] + gram_pair[...]

    def gram_rows(ax):
        return pl.ds(pl.multiple_of(core * 128 + ax * 32, 32), 32)

    at_x = gram_rows(x)
    gram_stage = {s: send(gram.at[gram_rows(mod4(x + s))], gram_x.at[s - 1], x_peer(s)) for s in (2, 1, 3)}
    a_right.wait_recv()
    piece = img.at[half_rows(3, 0)]
    opp_a = send(piece, piece, x_peer(1))
    b_left.wait_recv()
    piece = img.at[half_rows(1, 1)]
    opp_b = send(piece, piece, x_peer(3))
    for copy in gram_stage.values():
        copy.wait_recv()
    gram_z[0] = gram[at_x, :] + gram_x[0] + gram_x[1] + gram_x[2]
    gram_stage = [send(gram_z.at[0], gram_z.at[s], z_peer(s)) for s in (2, 1, 3)]
    for copy in (a_left, b_right, opp_a, opp_b):
        copy.wait_recv()

    img_t[...] = img[...].T

    def partial(off, part):
        cols = pl.ds(pl.multiple_of(off + part * PART, 128), PART)
        return dot(img_t[...], w_ref[:, cols])

    copies = []
    for part in (0, 1):
        mate_send[part] = partial(mate_off2, part).astype(BF16)
        copies.append(send(mate_send.at[part], mate_recv.at[part], mate))
    for copy in gram_stage:
        copy.wait_recv()
    gram_y[0] = gram_z[0] + gram_z[1] + gram_z[2] + gram_z[3]
    gram_stage = [send(gram_y.at[0], gram_y.at[s], y_peer(s)) for s in (2, 1, 3)]
    for part in (0, 1):
        value = partial(my_off2, part)
        copies[part].wait_recv()
        value = value + mate_recv[part].astype(F32)
        for tile in range(PART // 128):
            block = value[:, tile * 128 : tile * 128 + 128]
            z_f[part * (PART // 128) + tile] = block
            z_b[part * (PART // 128) + tile] = block.astype(BF16)

    scatter = {}
    for s in (2, 1, 3):
        a1 = mod4(p1 + s)
        for a2 in range(RING):
            scatter[s, a2] = send(z_b.at[a1 * s1 + a2 * s2], z_in.at[s - 1, a2], chip_peer(a1, p2))
    for copy in gram_stage:
        copy.wait_recv()
    total[at_x, :] = gram_y[0] + gram_y[1] + gram_y[2] + gram_y[3]
    gram_stage = [send(total.at[at_x], total.at[at_x], x_peer(s)) for s in (2, 1, 3)]
    for copy in gram_stage:
        copy.wait_recv()
    rows = pl.ds(g_core, 128)
    copy = send(total.at[rows], total.at[rows], mate)
    copy.wait_recv()

    whole = total[...]
    diagonal = lax.broadcasted_iota(jnp.int32, (RANK, RANK), 0) == lax.broadcasted_iota(
        jnp.int32, (RANK, RANK), 1
    )
    trace = jnp.sum(jnp.where(diagonal, whole, 0.0), keepdims=True)
    poly[pl.ds(0, RANK), :] = whole / trace
    poly[pl.ds(RANK, RANK), :] = jnp.where(diagonal, 1.0 / jnp.sqrt(trace), 0.0)

    def factor(g):
        return jnp.where(diagonal, 1.5, 0.0) - 0.5 * g

    def iteration(_, carry):
        both = poly[...]
        p = factor(both[:RANK])
        p_high, p_low = split(p)

        def times_p(a):
            a_high, a_low = split(a)
            return dot(a_high, p_high) + (dot(a_high, p_low) + dot(a_low, p_high))

        both = times_p(both)
        poly[pl.ds(RANK, RANK), :] = both[RANK:]
        poly[pl.ds(0, RANK), :] = times_p(both[:RANK])
        return carry

    lax.fori_loop(0, 2, iteration, 0)

    def row_sum(a2):
        for s in (1, 2, 3):
            scatter[s, a2].wait_recv()

    for a2 in range(RING):
        row_sum(a2)
        value = z_f[p1 * s1 + a2 * s2]
        for s in (1, 2, 3):
            value = value + z_in[s - 1, a2].astype(F32)
        row_f[a2] = value
        row_b[a2] = value.astype(BF16)
    column = [
        send(row_b.at[mod4(p2 + s)], col_in.at[s - 1], chip_peer(p1, mod4(p2 + s))) for s in (2, 1, 3)
    ]
    lax.fori_loop(2, ITERS - 1, iteration, 0)
    q = dot_split(poly[pl.ds(RANK, RANK), :], factor(poly[pl.ds(0, RANK), :]))
    for copy in column:
        copy.wait_recv()
    mine = row_f[p2]
    for s in range(3):
        mine = mine + col_in[s].astype(F32)
    coef[chip] = dot_split(q, mine).astype(BF16)

    q_high, q_low = split(q)

    def coef_block(a2, a1):
        return coef.at[a1 * s1 + a2 * s2]

    def share_coef(a2, a1):
        at = a1 * s1 + a2 * s2
        return send(coef.at[at], coef_mate.at[at], mate)

    def basis_rows():
        basis[...] = (dot(img[...], q_high) + dot(img[...], q_low)).astype(BF16)
        save = pltpu.make_async_copy(basis.at[pl.ds(0, ROWS)], basis_out, local_sem.at[1])
        save.start()
        return save

    gather16(coef_block, axis2, axis1, share_coef)
    save_basis = basis_rows()
    save_own = pltpu.make_async_copy(coef, coef_out.at[core], local_sem.at[2])
    save_mate = pltpu.make_async_copy(coef_mate, coef_out.at[1 - core], local_sem.at[3])
    save_own.start()
    save_mate.start()
    save_basis.wait()
    save_own.wait()
    save_mate.wait()
    assert count[0] <= COPIES, count[0]


COPIES = 128


def residual_kernel(w_ref, basis_ref, coef_ref, residual_ref, own_ref, whole):
    @pl.when(pl.program_id(0) == 0)
    def _():
        for tile in range(COLS // 128):
            at = (0, tile) if tile < TILES else (1, tile - SKIP2 // 128)
            whole[:, tile * 128 : tile * 128 + 128] = coef_ref[at]
        wide = lax.axis_index("wide")
        block = whole[pl.ds(pl.multiple_of((wide // 2) * BLK, BLK), BLK), :].astype(F32)
        first = lax.rem(wide, 2) == 0
        own_ref[...] = jnp.where(first, block[:8], block[8:]).astype(BF16)

    product = dot(basis_ref[...], whole[...])
    residual_ref[...] = (w_ref[...].astype(F32) - product).astype(BF16)


def shards(weight, sketch):
    basis, coef = pl.pallas_call(
        main_kernel,
        out_shape=(
            jax.ShapeDtypeStruct((ROWS, RANK), BF16),
            jax.ShapeDtypeStruct((2, TILES, RANK, 128), BF16),
        ),
        in_specs=[pl.BlockSpec(memory_space=pl.ANY), pl.BlockSpec(memory_space=pltpu.VMEM)],
        out_specs=[pl.BlockSpec(memory_space=pl.ANY)] * 2,
        scratch_shapes=[
            pltpu.VMEM((PAD, COLS), BF16),
            pltpu.VMEM((8, COLS), F32),
            pltpu.VMEM((8, WIDE), F32),
            pltpu.VMEM((RANK, COLS), BF16),
            pltpu.VMEM((PAD, RANK), F32),
            pltpu.VMEM((PAD, RANK), BF16),
            pltpu.VMEM((6, HALF, RANK), BF16),
            pltpu.VMEM((2, HALF, RANK), BF16),
            pltpu.VMEM((RANK, RANK), F32),
            pltpu.VMEM((RANK, RANK), F32),
            pltpu.VMEM((128, RANK), F32),
            pltpu.VMEM((3, 32, RANK), F32),
            pltpu.VMEM((4, 32, RANK), F32),
            pltpu.VMEM((4, 32, RANK), F32),
            pltpu.VMEM((2 * RANK, RANK), F32),
            pltpu.VMEM((PAD, RANK), BF16),
            pltpu.VMEM((PAD, RANK), BF16),
            pltpu.VMEM((RANK, PAD), BF16),
            pltpu.VMEM((2, RANK, PART), BF16),
            pltpu.VMEM((2, RANK, PART), BF16),
            pltpu.VMEM((TILES, RANK, 128), F32),
            pltpu.VMEM((TILES, RANK, 128), BF16),
            pltpu.VMEM((3, RING, RANK, 128), BF16),
            pltpu.VMEM((RING, RANK, 128), F32),
            pltpu.VMEM((RING, RANK, 128), BF16),
            pltpu.VMEM((3, RANK, 128), BF16),
            pltpu.VMEM((TILES, RANK, 128), BF16),
            pltpu.VMEM((TILES, RANK, 128), BF16),
            pltpu.SemaphoreType.DMA((4,)),
            pltpu.SemaphoreType.DMA((COPIES,)),
            pltpu.SemaphoreType.DMA((COPIES,)),
        ],
        compiler_params=pltpu.CompilerParams(
            collective_id=0, has_side_effects=True, vmem_limit_bytes=44 * 1024 * 1024
        ),
        cost_estimate=pl.CostEstimate(
            flops=2 * 2 * ROWS * COLS * RANK, bytes_accessed=2 * ROWS * COLS, transcendentals=0
        ),
        name="polar_basis",
    )(weight, sketch.T)

    rows = 240
    residual, own = pl.pallas_call(
        residual_kernel,
        grid=(pl.cdiv(ROWS, rows),),
        out_shape=(
            jax.ShapeDtypeStruct((ROWS, COLS), BF16),
            jax.ShapeDtypeStruct((8, COLS), BF16),
        ),
        in_specs=[
            pl.BlockSpec((rows, COLS), lambda i: (i, 0)),
            pl.BlockSpec((rows, RANK), lambda i: (i, 0)),
            pl.BlockSpec((2, TILES, RANK, 128), lambda i: (0, 0, 0, 0)),
        ],
        out_specs=[
            pl.BlockSpec((rows, COLS), lambda i: (i, 0)),
            pl.BlockSpec((8, COLS), lambda i: (0, 0)),
        ],
        scratch_shapes=[pltpu.VMEM((RANK, COLS), BF16)],
        compiler_params=pltpu.CompilerParams(vmem_limit_bytes=24 * 1024 * 1024),
        cost_estimate=pl.CostEstimate(
            flops=2 * ROWS * COLS * RANK, bytes_accessed=4 * ROWS * COLS, transcendentals=0
        ),
        name="residual",
    )(weight, basis, coef)
    return own, residual


def solution(mesh):
    placed = (P("wide", "narrow"), P("narrow", "wide"))
    return jax.shard_map(
        shards,
        mesh=mesh,
        in_specs=placed,
        out_specs=(P("wide", "narrow"), P("wide", "narrow")),
        check_vma=False,
    )
```

time: 113 us -> 87.3 us (0.77)
  Pallas kernels: 111 us -> 85.5 us
    pallas_call x1, Pallas kernels: 104 us -> 78.9 us  [shards(): pl.pallas_call(main_kernel, out_shape=(jax.ShapeDtypeStruct((ROWS, RANK),...]
where the time goes in v2:
time: 87.3 us; the launch traced here: 87.2 us
  Pallas kernels  85.5 us (98%)
  local copies, waits for them, and re-layouts  0.98 us (1%)
    pallas_call x1, Pallas kernels, shards(): pl.pallas_call(main_kernel, out_shape=(jax.ShapeDtypeStruct((ROWS, RANK),...  78.9 us
    pallas_call x1, Pallas kernels, shards(): pl.pallas_call(residual_kernel, grid=(pl.cdiv(ROWS, rows),), out_shape=(j...  6.69 us

profile of v2, /device:TPU:1, one launch (start us, length us, event | category | flops | bytes accessed | tf_op | source)
XLA Modules:
  0.0 87.2 jit_solution(3469064713049248052)
XLA Ops:
  0.6 0.0 slice-start
  0.6 0.0 copy-start
  0.6 1.0 %copy-done = bf16[3712,8]{0,1:T(8,128)(2,1)S(1)} copy-done((bf16[3712,8]{0,1:T(8,128)(2,1)S(1)}, bf16[3712,8]{0,1:T(8,128)(2,1)}, u32[]{:S(2)}) %copy-start) | copy-done | bytes 59416
  1.6 0.0 slice-start.1
  1.6 0.0 slice-start.2
  1.6 78.9 %polar_basis.1 = (bf16[1392,256]{1,0:T(8,128)(2,1)S(1)}, bf16[2,16,256,128]{3,2,1,0:T(8,128)(2,1)S(1)}) custom-call(bf16[1392,3712]{1,0:T(8,128)(2,1)} %w_ref.1, bf16[8,3712]{1,0:T(8,128)(2,1)S(1)} %bitcast.3), custom_call_target="tpu_custom_call" | custom-call | flops 5291114496 | bytes 10334208 | tf_op jit(solution)/shard_map/polar_basis/pallas_call | solution.py:393
  80.5 0.0 slice-done
  80.5 0.0 slice-done.1
  80.5 0.0 slice-done.2
  80.5 6.7 %residual.1 = (bf16[1392,3712]{1,0:T(8,128)(2,1)}, bf16[8,3712]{1,0:T(8,128)(2,1)}) custom-call(bf16[1392,3712]{1,0:T(8,128)(2,1)S(1)} %bitcast.2, bf16[1392,256]{1,0:T(8,128)(2,1)S(1)} %get-tuple-element.6.basis_ref, bf16[2,16,256,128]{3,2,1,0:T(8,128)(2,1)S(1)} %get-tuple-element.7.coef_ref), custom_call_target="tpu_custom_call" | custom-call | flops 2645557248 | bytes 20668416 | tf_op jit(solution)/shard_map/residual/pallas_call | solution.py:444
  (1 shorter events, 0.0 us)
Async XLA Ops:
  0.6 79.9 %slice-start = ((s8[10334208]{0:T(1024)(128)(4,1)}), s8[4194304]{0:T(1024)(128)(4,1)S(1)}, s32[]{:S(2)}) async-start(s8[10334208]{0:T(1024)(128)(4,1)} %bitcast.1), calls=%async_computation | async-start | bytes 8388608
  0.6 1.0 %copy-start = (bf16[3712,8]{0,1:T(8,128)(2,1)S(1)}, bf16[3712,8]{0,1:T(8,128)(2,1)}, u32[]{:S(2)}) copy-start(bf16[3712,8]{0,1:T(8,128)(2,1)} %param.3) | copy-start | bytes 178180
  1.6 78.9 %slice-start.1 = ((s8[10334208]{0:T(1024)(128)(4,1)}), s8[4194304]{0:T(1024)(128)(4,1)S(1)}, s32[]{:S(2)}) async-start(s8[10334208]{0:T(1024)(128)(4,1)} %bitcast.1), calls=%async_computation.1 | async-start | bytes 8388608
  1.6 78.9 %slice-start.2 = ((s8[10334208]{0:T(1024)(128)(4,1)}), s8[1945600]{0:T(1024)(128)(4,1)S(1)}, s32[]{:S(2)}) async-start(s8[10334208]{0:T(1024)(128)(4,1)} %bitcast.1), calls=%async_computation.2 | async-start | bytes 3891200

commit v3 on v2

--- a/solution.py
+++ b/solution.py
@@ -12,7 +12,7 @@
 COLS = 3712
 PAD = 1408
 CHUNK = PAD // RING
-HALF = CHUNK // 2
+STREAMS = ((0, 192), (192, 160))
 BLK = 16
 WIDE = 1920
 SKIP = COLS - WIDE
@@ -45,10 +45,11 @@
 
 def main_kernel(
     w_hbm,
-    sk_ref,
+    sk_hbm,
     basis_out,
     coef_out,
     w_ref,
+    sk_ref,
     own_sk,
     mate_sk,
     s_ref,
@@ -101,6 +102,8 @@
     def x_peer(step):
         return {"narrow": mod4(x + step)}
 
+    load_sk = pltpu.make_async_copy(sk_hbm, sk_ref, local_sem.at[1])
+    load_sk.start()
     load_w = pltpu.make_async_copy(w_hbm, w_ref.at[pl.ds(0, ROWS)], local_sem.at[0])
     load_w.start()
 
@@ -108,6 +111,7 @@
     peers = [mate] + [f(s) for f in (x_peer, y_peer, z_peer) for s in (1, 2, 3)]
     for peer in peers:
         pl.semaphore_signal(barrier, inc=1, device_id=peer, device_id_type=MESH)
+    load_sk.wait()
     own_sk[...] = sk_ref[...].astype(F32)
     w_ref[pl.ds(ROWS, PAD - ROWS), :] = jnp.zeros((PAD - ROWS, COLS), BF16)
     pl.semaphore_wait(barrier, len(peers))
@@ -135,7 +139,7 @@
             copy.wait_send()
         pending.clear()
 
-    def gather16(blk, u, v, share):
+    def gather16(blk, u, v, share, meanwhile):
         (pu, su), (pv, sv) = u, v
 
         def at_u(step):
@@ -158,6 +162,7 @@
             for t in (1, 3, 2):
                 copies[t].wait_recv()
                 shared.append(share(a, mod4(pv + 4 - t)))
+        meanwhile()
         for copy in shared:
             copy.wait_recv()
         drain()
@@ -184,57 +189,92 @@
         block = s_ref.at[rows, pl.ds(pl.multiple_of(only_off, 128), SKIP)]
         return send(block, block, mate)
 
-    gather16(sketch_block, axis1, axis2, share_sketch)
-    load_w.wait()
-
-    def chunk_rows(step):
-        return pl.multiple_of(mod4(x + step) * CHUNK, 16)
-
-    def image_chunk(step):
-        start = chunk_rows(step)
-        value = lax.dot_general(
-            w_ref[pl.ds(start, CHUNK), :],
-            s_ref[...],
+    def rows_dot(rows, off, start, width):
+        return lax.dot_general(
+            w_ref[rows, pl.ds(pl.multiple_of(off + start, 128), width)],
+            s_ref[:, pl.ds(pl.multiple_of(off + start, 128), width)],
             (((1,), (1,)), ((), ())),
             preferred_element_type=F32,
         )
-        part_f[pl.ds(start, CHUNK), :] = value
-        part_b[pl.ds(start, CHUNK), :] = value.astype(BF16)
-
-    def half_rows(step, second):
-        return pl.ds(pl.multiple_of(chunk_rows(step) + second * HALF, 16), HALF)
-
-    image_chunk(2)
-    in0 = send(part_b.at[half_rows(2, 0)], img_in.at[0], x_peer(1))
-    in1 = send(part_b.at[half_rows(2, 1)], img_in.at[1], x_peer(3))
-    image_chunk(1)
-    in2 = send(part_b.at[half_rows(1, 1)], img_in.at[2], x_peer(1))
-    image_chunk(3)
-    in3 = send(part_b.at[half_rows(3, 0)], img_in.at[3], x_peer(3))
-    in0.wait_recv()
-    img_mid[0] = (part_f[half_rows(1, 0), :] + img_in[0].astype(F32)).astype(BF16)
-    in4 = send(img_mid.at[0], img_in.at[4], x_peer(1))
-    in1.wait_recv()
-    img_mid[1] = (part_f[half_rows(3, 1), :] + img_in[1].astype(F32)).astype(BF16)
-    in5 = send(img_mid.at[1], img_in.at[5], x_peer(3))
-    image_chunk(0)
-    in3.wait_recv()
-    in4.wait_recv()
-    own_a, own_b = half_rows(0, 0), half_rows(0, 1)
-    img[own_a, :] = (part_f[own_a, :] + img_in[3].astype(F32) + img_in[4].astype(F32)).astype(BF16)
-    a_right = send(img.at[own_a], img.at[own_a], x_peer(1))
-    in2.wait_recv()
-    in5.wait_recv()
-    img[own_b, :] = (part_f[own_b, :] + img_in[2].astype(F32) + img_in[5].astype(F32)).astype(BF16)
-    b_left = send(img.at[own_b], img.at[own_b], x_peer(3))
-    b_right = send(img.at[own_b], img.at[own_b], x_peer(1))
-    a_left = send(img.at[own_a], img.at[own_a], x_peer(3))
-
-    own = img[pl.ds(chunk_rows(0), CHUNK), :]
+
+    def own_columns():
+        load_w.wait()
+        part_f[...] = rows_dot(pl.ds(0, PAD), my_off, 0, WIDE)
+
+    gather16(sketch_block, axis1, axis2, share_sketch, own_columns)
+    mate_only = (1 - core) * WIDE
+
+    def piece(step, start, size):
+        return pl.ds(pl.multiple_of(mod4(x + step) * CHUNK + start, 16), size)
+
+    def add_columns(step, start, size):
+        rows = piece(step, start, size)
+        value = part_f[rows, :] + rows_dot(rows, mate_only, 0, SKIP)
+        part_f[rows, :] = value
+        part_b[rows, :] = value.astype(BF16)
+
+    phase = []
+    for start, size in STREAMS:
+        for step in (2, 1, 3):
+            add_columns(step, start, size)
+            half = size // 2
+            a, b = piece(step, start, half), piece(step, start + half, half)
+            if step == 2:
+                n = len(phase)
+                one = {"a": lambda k, n=n, half=half: img_in.at[n, k, pl.ds(0, half)], "half": half, "start": start}
+                phase.append(one)
+                one[0] = send(part_b.at[a], one["a"](0), x_peer(1))
+                one[1] = send(part_b.at[b], one["a"](1), x_peer(3))
+            elif step == 1:
+                one[2] = send(part_b.at[b], one["a"](2), x_peer(1))
+            else:
+                one[3] = send(part_b.at[a], one["a"](3), x_peer(3))
+    for start, size in STREAMS:
+        add_columns(0, start, size)
+
+    def inbox(one, n, k):
+        return img_in[n, k, pl.ds(0, one["half"]), :].astype(F32)
+
+    for n, one in enumerate(phase):
+        start, half = one["start"], one["half"]
+        middle = pl.ds(0, half)
+        one[0].wait_recv()
+        img_mid[n, 0, middle, :] = (part_f[piece(1, start, half), :] + inbox(one, n, 0)).astype(BF16)
+        one[4] = send(img_mid.at[n, 0, middle], one["a"](4), x_peer(1))
+        one[1].wait_recv()
+        img_mid[n, 1, middle, :] = (part_f[piece(3, start + half, half), :] + inbox(one, n, 1)).astype(BF16)
+        one[5] = send(img_mid.at[n, 1, middle], one["a"](5), x_peer(3))
+
+    for n, one in enumerate(phase):
+        start, half = one["start"], one["half"]
+        own_a, own_b = piece(0, start, half), piece(0, start + half, half)
+        one[3].wait_recv()
+        one[4].wait_recv()
+        img[own_a, :] = (part_f[own_a, :] + inbox(one, n, 3) + inbox(one, n, 4)).astype(BF16)
+        one["a_right"] = send(img.at[own_a], img.at[own_a], x_peer(1))
+        one[2].wait_recv()
+        one[5].wait_recv()
+        img[own_b, :] = (part_f[own_b, :] + inbox(one, n, 2) + inbox(one, n, 5)).astype(BF16)
+        one["b_left"] = send(img.at[own_b], img.at[own_b], x_peer(3))
+        one["b_right"] = send(img.at[own_b], img.at[own_b], x_peer(1))
+        one["a_left"] = send(img.at[own_a], img.at[own_a], x_peer(3))
+
+    def pass_on(one):
+        start, half = one["start"], one["half"]
+        one["a_right"].wait_recv()
+        rows = piece(3, start, half)
+        one["opp_a"] = send(img.at[rows], img.at[rows], x_peer(1))
+        one["b_left"].wait_recv()
+        rows = piece(1, start + half, half)
+        one["opp_b"] = send(img.at[rows], img.at[rows], x_peer(3))
+
+    own = img[piece(0, 0, CHUNK), :]
     gram[...] = lax.dot_general(own, own, (((0,), (0,)), ((), ())), preferred_element_type=F32)
     g_core = pl.multiple_of(core * 128, 128)
     g_mate = pl.multiple_of((1 - core) * 128, 128)
     copy = send(gram.at[pl.ds(g_mate, 128)], gram_pair, mate)
+    for one in phase[:-1]:
+        pass_on(one)
     copy.wait_recv()
     gram[pl.ds(g_core, 128), :] = gram[pl.ds(g_core, 128), :] + gram_pair[...]
 
@@ -243,18 +283,14 @@
 
     at_x = gram_rows(x)
     gram_stage = {s: send(gram.at[gram_rows(mod4(x + s))], gram_x.at[s - 1], x_peer(s)) for s in (2, 1, 3)}
-    a_right.wait_recv()
-    piece = img.at[half_rows(3, 0)]
-    opp_a = send(piece, piece, x_peer(1))
-    b_left.wait_recv()
-    piece = img.at[half_rows(1, 1)]
-    opp_b = send(piece, piece, x_peer(3))
+    pass_on(phase[-1])
     for copy in gram_stage.values():
         copy.wait_recv()
     gram_z[0] = gram[at_x, :] + gram_x[0] + gram_x[1] + gram_x[2]
     gram_stage = [send(gram_z.at[0], gram_z.at[s], z_peer(s)) for s in (2, 1, 3)]
-    for copy in (a_left, b_right, opp_a, opp_b):
-        copy.wait_recv()
+    for one in phase:
+        for name in ("a_left", "b_right", "opp_a", "opp_b"):
+            one[name].wait_recv()
 
     img_t[...] = img[...].T
 
@@ -266,10 +302,6 @@
     for part in (0, 1):
         mate_send[part] = partial(mate_off2, part).astype(BF16)
         copies.append(send(mate_send.at[part], mate_recv.at[part], mate))
-    for copy in gram_stage:
-        copy.wait_recv()
-    gram_y[0] = gram_z[0] + gram_z[1] + gram_z[2] + gram_z[3]
-    gram_stage = [send(gram_y.at[0], gram_y.at[s], y_peer(s)) for s in (2, 1, 3)]
     for part in (0, 1):
         value = partial(my_off2, part)
         copies[part].wait_recv()
@@ -278,6 +310,11 @@
             block = value[:, tile * 128 : tile * 128 + 128]
             z_f[part * (PART // 128) + tile] = block
             z_b[part * (PART // 128) + tile] = block.astype(BF16)
+
+    for copy in gram_stage:
+        copy.wait_recv()
+    gram_y[0] = gram_z[0] + gram_z[1] + gram_z[2] + gram_z[3]
+    gram_stage = [send(gram_y.at[0], gram_y.at[s], y_peer(s)) for s in (2, 1, 3)]
 
     scatter = {}
     for s in (2, 1, 3):
@@ -294,33 +331,6 @@
     copy = send(total.at[rows], total.at[rows], mate)
     copy.wait_recv()
 
-    whole = total[...]
-    diagonal = lax.broadcasted_iota(jnp.int32, (RANK, RANK), 0) == lax.broadcasted_iota(
-        jnp.int32, (RANK, RANK), 1
-    )
-    trace = jnp.sum(jnp.where(diagonal, whole, 0.0), keepdims=True)
-    poly[pl.ds(0, RANK), :] = whole / trace
-    poly[pl.ds(RANK, RANK), :] = jnp.where(diagonal, 1.0 / jnp.sqrt(trace), 0.0)
-
-    def factor(g):
-        return jnp.where(diagonal, 1.5, 0.0) - 0.5 * g
-
-    def iteration(_, carry):
-        both = poly[...]
-        p = factor(both[:RANK])
-        p_high, p_low = split(p)
-
-        def times_p(a):
-            a_high, a_low = split(a)
-            return dot(a_high, p_high) + (dot(a_high, p_low) + dot(a_low, p_high))
-
-        both = times_p(both)
-        poly[pl.ds(RANK, RANK), :] = both[RANK:]
-        poly[pl.ds(0, RANK), :] = times_p(both[:RANK])
-        return carry
-
-    lax.fori_loop(0, 2, iteration, 0)
-
     def row_sum(a2):
         for s in (1, 2, 3):
             scatter[s, a2].wait_recv()
@@ -335,7 +345,33 @@
     column = [
         send(row_b.at[mod4(p2 + s)], col_in.at[s - 1], chip_peer(p1, mod4(p2 + s))) for s in (2, 1, 3)
     ]
-    lax.fori_loop(2, ITERS - 1, iteration, 0)
+
+    whole = total[...]
+    diagonal = lax.broadcasted_iota(jnp.int32, (RANK, RANK), 0) == lax.broadcasted_iota(
+        jnp.int32, (RANK, RANK), 1
+    )
+    trace = jnp.sum(jnp.where(diagonal, whole, 0.0), keepdims=True)
+    poly[pl.ds(0, RANK), :] = whole / trace
+    poly[pl.ds(RANK, RANK), :] = jnp.where(diagonal, 1.0 / jnp.sqrt(trace), 0.0)
+
+    def factor(g):
+        return jnp.where(diagonal, 1.5, 0.0) - 0.5 * g
+
+    def iteration(_, carry):
+        both = poly[...]
+        p = factor(both[:RANK])
+        p_high, p_low = split(p)
+
+        def times_p(a):
+            a_high, a_low = split(a)
+            return dot(a_high, p_high) + (dot(a_high, p_low) + dot(a_low, p_high))
+
+        both = times_p(both)
+        poly[pl.ds(RANK, RANK), :] = both[RANK:]
+        poly[pl.ds(0, RANK), :] = times_p(both[:RANK])
+        return carry
+
+    lax.fori_loop(0, ITERS - 1, iteration, 0)
     q = dot_split(poly[pl.ds(RANK, RANK), :], factor(poly[pl.ds(0, RANK), :]))
     for copy in column:
         copy.wait_recv()
@@ -359,8 +395,9 @@
         save.start()
         return save
 
-    gather16(coef_block, axis2, axis1, share_coef)
-    save_basis = basis_rows()
+    saved = []
+    gather16(coef_block, axis2, axis1, share_coef, lambda: saved.append(basis_rows()))
+    save_basis = saved[0]
     save_own = pltpu.make_async_copy(coef, coef_out.at[core], local_sem.at[2])
     save_mate = pltpu.make_async_copy(coef_mate, coef_out.at[1 - core], local_sem.at[3])
     save_own.start()
@@ -371,22 +408,31 @@
     assert count[0] <= COPIES, count[0]
 
 
-COPIES = 128
-
-
-def residual_kernel(w_ref, basis_ref, coef_ref, residual_ref, own_ref, whole):
-    @pl.when(pl.program_id(0) == 0)
-    def _():
-        for tile in range(COLS // 128):
-            at = (0, tile) if tile < TILES else (1, tile - SKIP2 // 128)
-            whole[:, tile * 128 : tile * 128 + 128] = coef_ref[at]
-        wide = lax.axis_index("wide")
-        block = whole[pl.ds(pl.multiple_of((wide // 2) * BLK, BLK), BLK), :].astype(F32)
-        first = lax.rem(wide, 2) == 0
-        own_ref[...] = jnp.where(first, block[:8], block[8:]).astype(BF16)
-
-    product = dot(basis_ref[...], whole[...])
-    residual_ref[...] = (w_ref[...].astype(F32) - product).astype(BF16)
+COPIES = 160
+STEP = 240
+
+
+def residual_kernel(w_ref, basis_ref, coef_ref, residual_out, own_ref, whole, result, sem):
+    for tile in range(COLS // 128):
+        at = (0, tile) if tile < TILES else (1, tile - SKIP2 // 128)
+        whole[:, tile * 128 : tile * 128 + 128] = coef_ref[at]
+    copies = []
+    for start in range(0, ROWS, STEP):
+        rows = pl.ds(start, min(STEP, ROWS - start))
+        left = basis_ref[rows, :]
+        for column in range(0, COLS, RANK):
+            cols = pl.ds(column, min(RANK, COLS - column))
+            value = w_ref[rows, cols].astype(F32) - dot(left, whole[:, cols])
+            result[rows, cols] = value.astype(BF16)
+        copy = pltpu.make_async_copy(result.at[rows], residual_out.at[rows], sem.at[len(copies)])
+        copy.start()
+        copies.append(copy)
+    wide = lax.axis_index("wide")
+    block = whole[pl.ds(pl.multiple_of((wide // 2) * BLK, BLK), BLK), :].astype(F32)
+    first = lax.rem(wide, 2) == 0
+    own_ref[...] = jnp.where(first, block[:8], block[8:]).astype(BF16)
+    for copy in copies:
+        copy.wait()
 
 
 def shards(weight, sketch):
@@ -396,17 +442,18 @@
             jax.ShapeDtypeStruct((ROWS, RANK), BF16),
             jax.ShapeDtypeStruct((2, TILES, RANK, 128), BF16),
         ),
-        in_specs=[pl.BlockSpec(memory_space=pl.ANY), pl.BlockSpec(memory_space=pltpu.VMEM)],
+        in_specs=[pl.BlockSpec(memory_space=pltpu.HBM)] * 2,
         out_specs=[pl.BlockSpec(memory_space=pl.ANY)] * 2,
         scratch_shapes=[
             pltpu.VMEM((PAD, COLS), BF16),
+            pltpu.VMEM((8, COLS), BF16),
             pltpu.VMEM((8, COLS), F32),
             pltpu.VMEM((8, WIDE), F32),
             pltpu.VMEM((RANK, COLS), BF16),
             pltpu.VMEM((PAD, RANK), F32),
             pltpu.VMEM((PAD, RANK), BF16),
-            pltpu.VMEM((6, HALF, RANK), BF16),
-            pltpu.VMEM((2, HALF, RANK), BF16),
+            pltpu.VMEM((len(STREAMS), 6, 96, RANK), BF16),
+            pltpu.VMEM((len(STREAMS), 2, 96, RANK), BF16),
             pltpu.VMEM((RANK, RANK), F32),
             pltpu.VMEM((RANK, RANK), F32),
             pltpu.VMEM((128, RANK), F32),
@@ -440,24 +487,22 @@
         name="polar_basis",
     )(weight, sketch.T)
 
-    rows = 240
     residual, own = pl.pallas_call(
         residual_kernel,
-        grid=(pl.cdiv(ROWS, rows),),
         out_shape=(
             jax.ShapeDtypeStruct((ROWS, COLS), BF16),
             jax.ShapeDtypeStruct((8, COLS), BF16),
         ),
-        in_specs=[
-            pl.BlockSpec((rows, COLS), lambda i: (i, 0)),
-            pl.BlockSpec((rows, RANK), lambda i: (i, 0)),
-            pl.BlockSpec((2, TILES, RANK, 128), lambda i: (0, 0, 0, 0)),
+        in_specs=[pl.BlockSpec(memory_space=pltpu.VMEM)] * 3,
+        out_specs=[
+            pl.BlockSpec(memory_space=pl.ANY),
+            pl.BlockSpec(memory_space=pltpu.VMEM),
         ],
-        out_specs=[
-            pl.BlockSpec((rows, COLS), lambda i: (i, 0)),
-            pl.BlockSpec((8, COLS), lambda i: (0, 0)),
+        scratch_shapes=[
+            pltpu.VMEM((RANK, COLS), BF16),
+            pltpu.VMEM((ROWS, COLS), BF16),
+            pltpu.SemaphoreType.DMA((pl.cdiv(ROWS, STEP),)),
         ],
-        scratch_shapes=[pltpu.VMEM((RANK, COLS), BF16)],
         compiler_params=pltpu.CompilerParams(vmem_limit_bytes=24 * 1024 * 1024),
         cost_estimate=pl.CostEstimate(
             flops=2 * ROWS * COLS * RANK, bytes_accessed=4 * ROWS * COLS, transcendentals=0

time: 87.3 us -> 84.1 us (0.963)
  Pallas kernels: 85.5 us -> 82.2 us
    pallas_call x1, Pallas kernels: 78.9 us -> 76.6 us  [shards(): pl.pallas_call(main_kernel, out_shape=(jax.ShapeDtypeStruct((ROWS, RANK),...]
    pallas_call x1, Pallas kernels: 6.69 us -> 5.56 us  [shards(): pl.pallas_call(residual_kernel, out_shape=(jax.ShapeDtypeStruct((ROWS, CO...]
where the time goes in v3:
time: 84.1 us; the launch traced here: 84 us
  Pallas kernels  82.2 us (98%)
  local copies, waits for them, and re-layouts  0.98 us (1%)
  between operations  0.85 us (1%)
    pallas_call x1, Pallas kernels, shards(): pl.pallas_call(main_kernel, out_shape=(jax.ShapeDtypeStruct((ROWS, RANK),...  76.6 us
    pallas_call x1, Pallas kernels, shards(): pl.pallas_call(residual_kernel, out_shape=(jax.ShapeDtypeStruct((ROWS, CO...  5.56 us

profile of v3, /device:TPU:1, one launch (start us, length us, event | category | flops | bytes accessed | tf_op | source)
XLA Modules:
  0.0 84.0 jit_solution(981159538556229148)
XLA Ops:
  0.6 0.0 slice-start
  0.6 0.0 copy-start
  0.6 1.0 %copy-done = bf16[3712,8]{0,1:T(8,128)(2,1)S(1)} copy-done((bf16[3712,8]{0,1:T(8,128)(2,1)S(1)}, bf16[3712,8]{0,1:T(8,128)(2,1)}, u32[]{:S(2)}) %copy-start) | copy-done | bytes 59416
  1.6 0.0 slice-start.1
  1.6 0.0 slice-start.2
  1.6 76.6 %polar_basis.1 = (bf16[1392,256]{1,0:T(8,128)(2,1)S(1)}, bf16[2,16,256,128]{3,2,1,0:T(8,128)(2,1)S(1)}) custom-call(bf16[1392,3712]{1,0:T(8,128)(2,1)} %w_ref.1, bf16[8,3712]{1,0:T(8,128)(2,1)S(1)} %bitcast.3), custom_call_target="tpu_custom_call" | custom-call | flops 5291114496 | bytes 10334208 | tf_op jit(solution)/shard_map/polar_basis/pallas_call | solution.py:439
  78.2 0.0 slice-done
  78.2 0.0 slice-done.1
  78.3 0.0 slice-done.2
  78.3 5.6 %residual.1 = (bf16[1392,3712]{1,0:T(8,128)(2,1)}, bf16[8,3712]{1,0:T(8,128)(2,1)}) custom-call(bf16[1392,3712]{1,0:T(8,128)(2,1)S(1)} %bitcast.2, bf16[1392,256]{1,0:T(8,128)(2,1)S(1)} %get-tuple-element.6.basis_ref, bf16[2,16,256,128]{3,2,1,0:T(8,128)(2,1)S(1)} %get-tuple-element.7.coef_ref), custom_call_target="tpu_custom_call" | custom-call | flops 2645557248 | bytes 20668416 | tf_op jit(solution)/shard_map/residual/pallas_call | solution.py:490
  (1 shorter events, 0.0 us)
Async XLA Ops:
  0.6 77.6 %slice-start = ((s8[10334208]{0:T(1024)(128)(4,1)}), s8[4194304]{0:T(1024)(128)(4,1)S(1)}, s32[]{:S(2)}) async-start(s8[10334208]{0:T(1024)(128)(4,1)} %bitcast.1), calls=%async_computation | async-start | bytes 8388608
  0.6 1.0 %copy-start = (bf16[3712,8]{0,1:T(8,128)(2,1)S(1)}, bf16[3712,8]{0,1:T(8,128)(2,1)}, u32[]{:S(2)}) copy-start(bf16[3712,8]{0,1:T(8,128)(2,1)} %param.3) | copy-start | bytes 178180
  1.6 76.6 %slice-start.1 = ((s8[10334208]{0:T(1024)(128)(4,1)}), s8[4194304]{0:T(1024)(128)(4,1)S(1)}, s32[]{:S(2)}) async-start(s8[10334208]{0:T(1024)(128)(4,1)} %bitcast.1), calls=%async_computation.1 | async-start | bytes 8388608
  1.6 76.6 %slice-start.2 = ((s8[10334208]{0:T(1024)(128)(4,1)}), s8[1945600]{0:T(1024)(128)(4,1)S(1)}, s32[]{:S(2)}) async-start(s8[10334208]{0:T(1024)(128)(4,1)} %bitcast.1), calls=%async_computation.2 | async-start | bytes 3891200

commit v4 on v3

--- a/solution.py
+++ b/solution.py
@@ -18,7 +18,6 @@
 SKIP = COLS - WIDE
 TILES = 16
 SKIP2 = COLS - TILES * 128
-PART = TILES * 64
 MESH = pl.DeviceIdType.MESH
 F32 = jnp.float32
 BF16 = jnp.bfloat16
@@ -64,7 +63,6 @@
     gram_y,
     gram_z,
     poly,
-    basis,
     img,
     img_t,
     mate_send,
@@ -75,8 +73,6 @@
     row_f,
     row_b,
     col_in,
-    coef,
-    coef_mate,
     local_sem,
     send_sem,
     recv_sem,
@@ -214,21 +210,20 @@
         part_b[rows, :] = value.astype(BF16)
 
     phase = []
-    for start, size in STREAMS:
-        for step in (2, 1, 3):
-            add_columns(step, start, size)
-            half = size // 2
-            a, b = piece(step, start, half), piece(step, start + half, half)
-            if step == 2:
-                n = len(phase)
-                one = {"a": lambda k, n=n, half=half: img_in.at[n, k, pl.ds(0, half)], "half": half, "start": start}
-                phase.append(one)
-                one[0] = send(part_b.at[a], one["a"](0), x_peer(1))
-                one[1] = send(part_b.at[b], one["a"](1), x_peer(3))
-            elif step == 1:
-                one[2] = send(part_b.at[b], one["a"](2), x_peer(1))
-            else:
-                one[3] = send(part_b.at[a], one["a"](3), x_peer(3))
+    for n, (start, size) in enumerate(STREAMS):
+        half = size // 2
+        one = {"start": start, "half": half}
+        one["in"] = [img_in.at[n, k, pl.ds(0, half)] for k in range(6)]
+        phase.append(one)
+        add_columns(2, start, size)
+        one[0] = send(part_b.at[piece(2, start, half)], one["in"][0], x_peer(1))
+        one[1] = send(part_b.at[piece(2, start + half, half)], one["in"][1], x_peer(3))
+    for one, (start, size) in zip(phase, STREAMS):
+        half = size // 2
+        add_columns(1, start, size)
+        one[2] = send(part_b.at[piece(1, start + half, half)], one["in"][2], x_peer(1))
+        add_columns(3, start, size)
+        one[3] = send(part_b.at[piece(3, start, half)], one["in"][3], x_peer(3))
     for start, size in STREAMS:
         add_columns(0, start, size)
 
@@ -240,10 +235,10 @@
         middle = pl.ds(0, half)
         one[0].wait_recv()
         img_mid[n, 0, middle, :] = (part_f[piece(1, start, half), :] + inbox(one, n, 0)).astype(BF16)
-        one[4] = send(img_mid.at[n, 0, middle], one["a"](4), x_peer(1))
+        one[4] = send(img_mid.at[n, 0, middle], one["in"][4], x_peer(1))
         one[1].wait_recv()
         img_mid[n, 1, middle, :] = (part_f[piece(3, start + half, half), :] + inbox(one, n, 1)).astype(BF16)
-        one[5] = send(img_mid.at[n, 1, middle], one["a"](5), x_peer(3))
+        one[5] = send(img_mid.at[n, 1, middle], one["in"][5], x_peer(3))
 
     for n, one in enumerate(phase):
         start, half = one["start"], one["half"]
@@ -294,57 +289,61 @@
 
     img_t[...] = img[...].T
 
-    def partial(off, part):
-        cols = pl.ds(pl.multiple_of(off + part * PART, 128), PART)
-        return dot(img_t[...], w_ref[:, cols])
-
+    def group(off, a2, sa, sb):
+        columns = [
+            w_ref[:, pl.ds(pl.multiple_of(off + (a1 * sa + a2 * sb) * 128, 128), 128)]
+            for a1 in range(RING)
+        ]
+        return dot(img_t[...], jnp.concatenate(columns, axis=1))
+
+    turns = (2, 1, 3, 0)
     copies = []
-    for part in (0, 1):
-        mate_send[part] = partial(mate_off2, part).astype(BF16)
-        copies.append(send(mate_send.at[part], mate_recv.at[part], mate))
-    for part in (0, 1):
-        value = partial(my_off2, part)
-        copies[part].wait_recv()
-        value = value + mate_recv[part].astype(F32)
-        for tile in range(PART // 128):
-            block = value[:, tile * 128 : tile * 128 + 128]
-            z_f[part * (PART // 128) + tile] = block
-            z_b[part * (PART // 128) + tile] = block.astype(BF16)
-
-    for copy in gram_stage:
-        copy.wait_recv()
-    gram_y[0] = gram_z[0] + gram_z[1] + gram_z[2] + gram_z[3]
-    gram_stage = [send(gram_y.at[0], gram_y.at[s], y_peer(s)) for s in (2, 1, 3)]
-
-    scatter = {}
-    for s in (2, 1, 3):
-        a1 = mod4(p1 + s)
-        for a2 in range(RING):
-            scatter[s, a2] = send(z_b.at[a1 * s1 + a2 * s2], z_in.at[s - 1, a2], chip_peer(a1, p2))
+    for j, s in enumerate(turns):
+        mate_send[j] = group(mate_off2, mod4(p1 + s), s2, s1).astype(BF16)
+        copies.append(send(mate_send.at[j], mate_recv.at[j], mate))
+
+    scatter = []
+    for j, s in enumerate(turns):
+        value = group(my_off2, mod4(p2 + s), s1, s2)
+        copies[j].wait_recv()
+        value = value + mate_recv[j].astype(F32)
+        for a1 in range(RING):
+            block = value[:, a1 * 128 : a1 * 128 + 128]
+            z_f[j, a1] = block
+            z_b[j, a1] = block.astype(BF16)
+        if j == 0:
+            for copy in gram_stage:
+                copy.wait_recv()
+            gram_y[0] = gram_z[0] + gram_z[1] + gram_z[2] + gram_z[3]
+            gram_stage = [send(gram_y.at[0], gram_y.at[t], y_peer(t)) for t in (2, 1, 3)]
+        peers_u = [(t, mod4(p1 + t)) for t in (2, 1, 3)]
+        scatter.append([send(z_b.at[j, a1], z_in.at[j, t - 1], chip_peer(a1, p2)) for t, a1 in peers_u])
+
+    def row_sum(j):
+        for copy in scatter[j]:
+            copy.wait_recv()
+        value = z_f[j, p1]
+        for t in range(3):
+            value = value + z_in[j, t].astype(F32)
+        return value
+
+    def send_row(j):
+        s = turns[j]
+        row_b[j] = row_sum(j).astype(BF16)
+        return send(row_b.at[j], col_in.at[s - 1], chip_peer(p1, mod4(p2 + s)))
+
     for copy in gram_stage:
         copy.wait_recv()
     total[at_x, :] = gram_y[0] + gram_y[1] + gram_y[2] + gram_y[3]
     gram_stage = [send(total.at[at_x], total.at[at_x], x_peer(s)) for s in (2, 1, 3)]
+    column = [send_row(0), send_row(1)]
     for copy in gram_stage:
         copy.wait_recv()
     rows = pl.ds(g_core, 128)
     copy = send(total.at[rows], total.at[rows], mate)
+    column.append(send_row(2))
+    row_f[...] = row_sum(3)
     copy.wait_recv()
-
-    def row_sum(a2):
-        for s in (1, 2, 3):
-            scatter[s, a2].wait_recv()
-
-    for a2 in range(RING):
-        row_sum(a2)
-        value = z_f[p1 * s1 + a2 * s2]
-        for s in (1, 2, 3):
-            value = value + z_in[s - 1, a2].astype(F32)
-        row_f[a2] = value
-        row_b[a2] = value.astype(BF16)
-    column = [
-        send(row_b.at[mod4(p2 + s)], col_in.at[s - 1], chip_peer(p1, mod4(p2 + s))) for s in (2, 1, 3)
-    ]
 
     whole = total[...]
     diagonal = lax.broadcasted_iota(jnp.int32, (RANK, RANK), 0) == lax.broadcasted_iota(
@@ -375,36 +374,24 @@
     q = dot_split(poly[pl.ds(RANK, RANK), :], factor(poly[pl.ds(0, RANK), :]))
     for copy in column:
         copy.wait_recv()
-    mine = row_f[p2]
+    mine = row_f[...]
     for s in range(3):
         mine = mine + col_in[s].astype(F32)
-    coef[chip] = dot_split(q, mine).astype(BF16)
+    coef_out[core, chip] = dot_split(q, mine).astype(BF16)
 
     q_high, q_low = split(q)
 
     def coef_block(a2, a1):
-        return coef.at[a1 * s1 + a2 * s2]
+        return coef_out.at[core, a1 * s1 + a2 * s2]
 
     def share_coef(a2, a1):
-        at = a1 * s1 + a2 * s2
-        return send(coef.at[at], coef_mate.at[at], mate)
+        return send(coef_block(a2, a1), coef_block(a2, a1), mate)
 
     def basis_rows():
-        basis[...] = (dot(img[...], q_high) + dot(img[...], q_low)).astype(BF16)
-        save = pltpu.make_async_copy(basis.at[pl.ds(0, ROWS)], basis_out, local_sem.at[1])
-        save.start()
-        return save
-
-    saved = []
-    gather16(coef_block, axis2, axis1, share_coef, lambda: saved.append(basis_rows()))
-    save_basis = saved[0]
-    save_own = pltpu.make_async_copy(coef, coef_out.at[core], local_sem.at[2])
-    save_mate = pltpu.make_async_copy(coef_mate, coef_out.at[1 - core], local_sem.at[3])
-    save_own.start()
-    save_mate.start()
-    save_basis.wait()
-    save_own.wait()
-    save_mate.wait()
+        own = img[pl.ds(0, ROWS), :]
+        basis_out[...] = (dot(own, q_high) + dot(own, q_low)).astype(BF16)
+
+    gather16(coef_block, axis2, axis1, share_coef, basis_rows)
     assert count[0] <= COPIES, count[0]
 
 
@@ -443,7 +430,7 @@
             jax.ShapeDtypeStruct((2, TILES, RANK, 128), BF16),
         ),
         in_specs=[pl.BlockSpec(memory_space=pltpu.HBM)] * 2,
-        out_specs=[pl.BlockSpec(memory_space=pl.ANY)] * 2,
+        out_specs=[pl.BlockSpec(memory_space=pltpu.VMEM)] * 2,
         scratch_shapes=[
             pltpu.VMEM((PAD, COLS), BF16),
             pltpu.VMEM((8, COLS), BF16),
@@ -462,19 +449,16 @@
             pltpu.VMEM((4, 32, RANK), F32),
             pltpu.VMEM((2 * RANK, RANK), F32),
             pltpu.VMEM((PAD, RANK), BF16),
-            pltpu.VMEM((PAD, RANK), BF16),
             pltpu.VMEM((RANK, PAD), BF16),
-            pltpu.VMEM((2, RANK, PART), BF16),
-            pltpu.VMEM((2, RANK, PART), BF16),
-            pltpu.VMEM((TILES, RANK, 128), F32),
-            pltpu.VMEM((TILES, RANK, 128), BF16),
-            pltpu.VMEM((3, RING, RANK, 128), BF16),
-            pltpu.VMEM((RING, RANK, 128), F32),
-            pltpu.VMEM((RING, RANK, 128), BF16),
+            pltpu.VMEM((RING, RANK, 512), BF16),
+            pltpu.VMEM((RING, RANK, 512), BF16),
+            pltpu.VMEM((RING, RING, RANK, 128), F32),
+            pltpu.VMEM((RING, RING, RANK, 128), BF16),
+            pltpu.VMEM((RING, 3, RANK, 128), BF16),
+            pltpu.VMEM((RANK, 128), F32),
             pltpu.VMEM((3, RANK, 128), BF16),
-            pltpu.VMEM((TILES, RANK, 128), BF16),
-            pltpu.VMEM((TILES, RANK, 128), BF16),
-            pltpu.SemaphoreType.DMA((4,)),
+            pltpu.VMEM((3, RANK, 128), BF16),
+            pltpu.SemaphoreType.DMA((2,)),
             pltpu.SemaphoreType.DMA((COPIES,)),
             pltpu.SemaphoreType.DMA((COPIES,)),
         ],

time: 84.1 us -> 82.7 us (0.983)
  Pallas kernels: 82.2 us -> 80.8 us
    pallas_call x1, Pallas kernels: 76.6 us -> 75.2 us  [shards(): pl.pallas_call(main_kernel, out_shape=(jax.ShapeDtypeStruct((ROWS, RANK),...]
where the time goes in v4:
time: 82.7 us; the launch traced here: 82.6 us
  Pallas kernels  80.8 us (98%)
  local copies, waits for them, and re-layouts  0.98 us (1%)
  between operations  0.85 us (1%)
    pallas_call x1, Pallas kernels, shards(): pl.pallas_call(main_kernel, out_shape=(jax.ShapeDtypeStruct((ROWS, RANK),...  75.2 us
    pallas_call x1, Pallas kernels, shards(): pl.pallas_call(residual_kernel, out_shape=(jax.ShapeDtypeStruct((ROWS, CO...  5.56 us

profile of v4, /device:TPU:1, one launch (start us, length us, event | category | flops | bytes accessed | tf_op | source)
XLA Modules:
  0.0 82.6 jit_solution(14859931655081609464)
XLA Ops:
  0.6 0.0 slice-start
  0.6 0.0 copy-start
  0.6 1.0 %copy-done = bf16[3712,8]{0,1:T(8,128)(2,1)S(1)} copy-done((bf16[3712,8]{0,1:T(8,128)(2,1)S(1)}, bf16[3712,8]{0,1:T(8,128)(2,1)}, u32[]{:S(2)}) %copy-start) | copy-done | bytes 59416
  1.6 0.0 slice-start.1
  1.6 0.0 slice-start.2
  1.6 75.2 %polar_basis.1 = (bf16[1392,256]{1,0:T(8,128)(2,1)S(1)}, bf16[2,16,256,128]{3,2,1,0:T(8,128)(2,1)S(1)}) custom-call(bf16[1392,3712]{1,0:T(8,128)(2,1)} %w_ref.1, bf16[8,3712]{1,0:T(8,128)(2,1)S(1)} %bitcast.3), custom_call_target="tpu_custom_call" | custom-call | flops 5291114496 | bytes 10334208 | tf_op jit(solution)/shard_map/polar_basis/pallas_call | solution.py:426
  76.8 0.0 slice-done
  76.9 0.0 slice-done.1
  76.9 0.0 slice-done.2
  76.9 5.6 %residual.1 = (bf16[1392,3712]{1,0:T(8,128)(2,1)}, bf16[8,3712]{1,0:T(8,128)(2,1)}) custom-call(bf16[1392,3712]{1,0:T(8,128)(2,1)S(1)} %bitcast.2, bf16[1392,256]{1,0:T(8,128)(2,1)S(1)} %get-tuple-element.6.basis_ref, bf16[2,16,256,128]{3,2,1,0:T(8,128)(2,1)S(1)} %get-tuple-element.7.coef_ref), custom_call_target="tpu_custom_call" | custom-call | flops 2645557248 | bytes 20668416 | tf_op jit(solution)/shard_map/residual/pallas_call | solution.py:474
  (1 shorter events, 0.0 us)
Async XLA Ops:
  0.6 76.2 %slice-start = ((s8[10334208]{0:T(1024)(128)(4,1)}), s8[4194304]{0:T(1024)(128)(4,1)S(1)}, s32[]{:S(2)}) async-start(s8[10334208]{0:T(1024)(128)(4,1)} %bitcast.1), calls=%async_computation | async-start | bytes 8388608
  0.6 1.0 %copy-start = (bf16[3712,8]{0,1:T(8,128)(2,1)S(1)}, bf16[3712,8]{0,1:T(8,128)(2,1)}, u32[]{:S(2)}) copy-start(bf16[3712,8]{0,1:T(8,128)(2,1)} %param.3) | copy-start | bytes 178180
  1.6 75.2 %slice-start.1 = ((s8[10334208]{0:T(1024)(128)(4,1)}), s8[4194304]{0:T(1024)(128)(4,1)S(1)}, s32[]{:S(2)}) async-start(s8[10334208]{0:T(1024)(128)(4,1)} %bitcast.1), calls=%async_computation.1 | async-start | bytes 8388608
  1.6 75.2 %slice-start.2 = ((s8[10334208]{0:T(1024)(128)(4,1)}), s8[1945600]{0:T(1024)(128)(4,1)S(1)}, s32[]{:S(2)}) async-start(s8[10334208]{0:T(1024)(128)(4,1)} %bitcast.1), calls=%async_computation.2 | async-start | bytes 3891200

commit v5 on v4

--- a/solution.py
+++ b/solution.py
@@ -57,6 +57,7 @@
     img_in,
     img_mid,
     gram,
+    gram_own,
     total,
     gram_pair,
     gram_x,
@@ -264,24 +265,27 @@
         one["opp_b"] = send(img.at[rows], img.at[rows], x_peer(3))
 
     own = img[piece(0, 0, CHUNK), :]
-    gram[...] = lax.dot_general(own, own, (((0,), (0,)), ((), ())), preferred_element_type=F32)
-    g_core = pl.multiple_of(core * 128, 128)
-    g_mate = pl.multiple_of((1 - core) * 128, 128)
-    copy = send(gram.at[pl.ds(g_mate, 128)], gram_pair, mate)
+    full = lax.dot_general(own, own, (((0,), (0,)), ((), ())), preferred_element_type=F32)
+    for c in (0, 1):
+        gram[c, pl.ds(0, 128), :] = full[c * 128 : c * 128 + 128, c * 128 : c * 128 + 128]
+        gram[c, pl.ds(128, 64), :] = full[c * 64 : c * 64 + 64, 128:]
+    copy = send(gram.at[1 - core], gram_pair, mate)
     for one in phase[:-1]:
         pass_on(one)
     copy.wait_recv()
-    gram[pl.ds(g_core, 128), :] = gram[pl.ds(g_core, 128), :] + gram_pair[...]
+    gram_own[...] = gram[core] + gram_pair[...]
 
     def gram_rows(ax):
-        return pl.ds(pl.multiple_of(core * 128 + ax * 32, 32), 32)
+        return pl.ds(pl.multiple_of(ax * 48, 16), 48)
 
     at_x = gram_rows(x)
-    gram_stage = {s: send(gram.at[gram_rows(mod4(x + s))], gram_x.at[s - 1], x_peer(s)) for s in (2, 1, 3)}
+    gram_stage = {
+        s: send(gram_own.at[gram_rows(mod4(x + s))], gram_x.at[s - 1], x_peer(s)) for s in (2, 1, 3)
+    }
     pass_on(phase[-1])
     for copy in gram_stage.values():
         copy.wait_recv()
-    gram_z[0] = gram[at_x, :] + gram_x[0] + gram_x[1] + gram_x[2]
+    gram_z[0] = gram_own[at_x, :] + gram_x[0] + gram_x[1] + gram_x[2]
     gram_stage = [send(gram_z.at[0], gram_z.at[s], z_peer(s)) for s in (2, 1, 3)]
     for one in phase:
         for name in ("a_left", "b_right", "opp_a", "opp_b"):
@@ -334,18 +338,21 @@
 
     for copy in gram_stage:
         copy.wait_recv()
-    total[at_x, :] = gram_y[0] + gram_y[1] + gram_y[2] + gram_y[3]
-    gram_stage = [send(total.at[at_x], total.at[at_x], x_peer(s)) for s in (2, 1, 3)]
+    total[core, at_x, :] = gram_y[0] + gram_y[1] + gram_y[2] + gram_y[3]
+    mine = total.at[core, at_x]
+    gram_stage = [send(mine, mine, x_peer(s)) for s in (2, 1, 3)]
     column = [send_row(0), send_row(1)]
     for copy in gram_stage:
         copy.wait_recv()
-    rows = pl.ds(g_core, 128)
-    copy = send(total.at[rows], total.at[rows], mate)
+    copy = send(total.at[core], total.at[core], mate)
     column.append(send_row(2))
     row_f[...] = row_sum(3)
     copy.wait_recv()
 
-    whole = total[...]
+    beside = jnp.concatenate([total[0, pl.ds(128, 64), :], total[1, pl.ds(128, 64), :]], axis=0)
+    top = jnp.concatenate([total[0, pl.ds(0, 128), :], beside], axis=1)
+    bottom = jnp.concatenate([beside.T, total[1, pl.ds(0, 128), :]], axis=1)
+    whole = jnp.concatenate([top, bottom], axis=0)
     diagonal = lax.broadcasted_iota(jnp.int32, (RANK, RANK), 0) == lax.broadcasted_iota(
         jnp.int32, (RANK, RANK), 1
     )
@@ -356,30 +363,33 @@
     def factor(g):
         return jnp.where(diagonal, 1.5, 0.0) - 0.5 * g
 
-    def iteration(_, carry):
-        both = poly[...]
-        p = factor(both[:RANK])
-        p_high, p_low = split(p)
+    def step(both):
+        p_high, p_low = split(factor(both[:RANK]))
 
         def times_p(a):
             a_high, a_low = split(a)
             return dot(a_high, p_high) + (dot(a_high, p_low) + dot(a_low, p_high))
 
         both = times_p(both)
-        poly[pl.ds(RANK, RANK), :] = both[RANK:]
-        poly[pl.ds(0, RANK), :] = times_p(both[:RANK])
+        return times_p(both[:RANK]), both[RANK:]
+
+    def iteration(_, carry):
+        g, q = step(poly[...])
+        poly[pl.ds(0, RANK), :] = g
+        poly[pl.ds(RANK, RANK), :] = q
         return carry
 
-    lax.fori_loop(0, ITERS - 1, iteration, 0)
-    q = dot_split(poly[pl.ds(RANK, RANK), :], factor(poly[pl.ds(0, RANK), :]))
+    lax.fori_loop(0, ITERS - 2, iteration, 0)
     for copy in column:
         copy.wait_recv()
     mine = row_f[...]
     for s in range(3):
         mine = mine + col_in[s].astype(F32)
-    coef_out[core, chip] = dot_split(q, mine).astype(BF16)
-
-    q_high, q_low = split(q)
+    g, q = step(poly[...])
+    last = factor(g)
+    coef_out[core, chip] = dot_split(last, dot_split(q, mine)).astype(BF16)
+    poly[pl.ds(0, RANK), :] = last
+    poly[pl.ds(RANK, RANK), :] = q
 
     def coef_block(a2, a1):
         return coef_out.at[core, a1 * s1 + a2 * s2]
@@ -389,6 +399,7 @@
 
     def basis_rows():
         own = img[pl.ds(0, ROWS), :]
+        q_high, q_low = split(dot_split(poly[pl.ds(RANK, RANK), :], poly[pl.ds(0, RANK), :]))
         basis_out[...] = (dot(own, q_high) + dot(own, q_low)).astype(BF16)
 
     gather16(coef_block, axis2, axis1, share_coef, basis_rows)
@@ -396,28 +407,33 @@
 
 
 COPIES = 160
-STEP = 240
-
-
-def residual_kernel(w_ref, basis_ref, coef_ref, residual_out, own_ref, whole, result, sem):
-    for tile in range(COLS // 128):
-        at = (0, tile) if tile < TILES else (1, tile - SKIP2 // 128)
-        whole[:, tile * 128 : tile * 128 + 128] = coef_ref[at]
+STEPS = (48, 96, 192, 240, 288, 288, 240)
+
+
+def residual_kernel(w_ref, basis_ref, coef_ref, residual_out, own_ref, result, sem):
+    def tile(at):
+        return coef_ref.at[(0, at) if at < TILES else (1, at - SKIP2 // 128)]
+
     copies = []
-    for start in range(0, ROWS, STEP):
-        rows = pl.ds(start, min(STEP, ROWS - start))
+    start = 0
+    for n, size in enumerate(STEPS):
+        rows = pl.ds(start, size)
         left = basis_ref[rows, :]
-        for column in range(0, COLS, RANK):
-            cols = pl.ds(column, min(RANK, COLS - column))
-            value = w_ref[rows, cols].astype(F32) - dot(left, whole[:, cols])
-            result[rows, cols] = value.astype(BF16)
-        copy = pltpu.make_async_copy(result.at[rows], residual_out.at[rows], sem.at[len(copies)])
+        for at in range(0, COLS // 128, 2):
+            width = min(2, COLS // 128 - at)
+            cols = pl.ds(at * 128, width * 128)
+            right = jnp.concatenate([tile(at + k)[...] for k in range(width)], axis=1)
+            result[rows, cols] = (w_ref[rows, cols].astype(F32) - dot(left, right)).astype(BF16)
+        copy = pltpu.make_async_copy(result.at[rows], residual_out.at[rows], sem.at[n])
         copy.start()
         copies.append(copy)
+        start += size
     wide = lax.axis_index("wide")
-    block = whole[pl.ds(pl.multiple_of((wide // 2) * BLK, BLK), BLK), :].astype(F32)
+    rows = pl.ds(pl.multiple_of((wide // 2) * BLK, BLK), BLK)
     first = lax.rem(wide, 2) == 0
-    own_ref[...] = jnp.where(first, block[:8], block[8:]).astype(BF16)
+    for at in range(COLS // 128):
+        block = tile(at)[rows, :].astype(F32)
+        own_ref[:, at * 128 : at * 128 + 128] = jnp.where(first, block[:8], block[8:]).astype(BF16)
     for copy in copies:
         copy.wait()
 
@@ -441,12 +457,13 @@
             pltpu.VMEM((PAD, RANK), BF16),
             pltpu.VMEM((len(STREAMS), 6, 96, RANK), BF16),
             pltpu.VMEM((len(STREAMS), 2, 96, RANK), BF16),
-            pltpu.VMEM((RANK, RANK), F32),
-            pltpu.VMEM((RANK, RANK), F32),
-            pltpu.VMEM((128, RANK), F32),
-            pltpu.VMEM((3, 32, RANK), F32),
-            pltpu.VMEM((4, 32, RANK), F32),
-            pltpu.VMEM((4, 32, RANK), F32),
+            pltpu.VMEM((2, 192, 128), F32),
+            pltpu.VMEM((192, 128), F32),
+            pltpu.VMEM((2, 192, 128), F32),
+            pltpu.VMEM((192, 128), F32),
+            pltpu.VMEM((3, 48, 128), F32),
+            pltpu.VMEM((4, 48, 128), F32),
+            pltpu.VMEM((4, 48, 128), F32),
             pltpu.VMEM((2 * RANK, RANK), F32),
             pltpu.VMEM((PAD, RANK), BF16),
             pltpu.VMEM((RANK, PAD), BF16),
@@ -469,7 +486,7 @@
             flops=2 * 2 * ROWS * COLS * RANK, bytes_accessed=2 * ROWS * COLS, transcendentals=0
         ),
         name="polar_basis",
-    )(weight, sketch.T)
+    )(weight, pltpu.with_memory_space_constraint(sketch.T, pltpu.HBM))
 
     residual, own = pl.pallas_call(
         residual_kernel,
@@ -483,9 +500,8 @@
             pl.BlockSpec(memory_space=pltpu.VMEM),
         ],
         scratch_shapes=[
-            pltpu.VMEM((RANK, COLS), BF16),
             pltpu.VMEM((ROWS, COLS), BF16),
-            pltpu.SemaphoreType.DMA((pl.cdiv(ROWS, STEP),)),
+            pltpu.SemaphoreType.DMA((len(STEPS),)),
         ],
         compiler_params=pltpu.CompilerParams(vmem_limit_bytes=24 * 1024 * 1024),
         cost_estimate=pl.CostEstimate(

time: 82.7 us -> 81.3 us (0.983)
  local copies, waits for them, and re-layouts: 0.98 us -> 0.01 us
    unnamed x8 -> x6, local copies, waits for them, and re-layouts: 0.98 us -> 0.01 us
where the time goes in v5:
time: 81.3 us; the launch traced here: 81.1 us
  Pallas kernels  80.3 us (99%)
  between operations  0.85 us (1%)
    pallas_call x1, Pallas kernels, shards(): pl.pallas_call(main_kernel, out_shape=(jax.ShapeDtypeStruct((ROWS, RANK),...  74.7 us
    pallas_call x1, Pallas kernels, shards(): pl.pallas_call(residual_kernel, out_shape=(jax.ShapeDtypeStruct((ROWS, CO...  5.59 us

profile of v5, /device:TPU:1, one launch (start us, length us, event | category | flops | bytes accessed | tf_op | source)
XLA Modules:
  0.0 81.1 jit_solution(8765274370452638729)
XLA Ops:
  0.6 0.0 slice-start
  0.6 0.0 slice-start.1
  0.7 0.0 slice-start.2
  0.7 74.7 %polar_basis.1 = (bf16[1392,256]{1,0:T(8,128)(2,1)S(1)}, bf16[2,16,256,128]{3,2,1,0:T(8,128)(2,1)S(1)}) custom-call(bf16[1392,3712]{1,0:T(8,128)(2,1)} %w_ref.1, bf16[8,3712]{1,0:T(8,128)(2,1)} %bitcast.3), custom_call_target="tpu_custom_call" | custom-call | flops 5291114496 | bytes 10334208 | tf_op jit(solution)/shard_map/polar_basis/pallas_call | solution.py:442
  75.4 0.0 slice-done
  75.4 0.0 slice-done.1
  75.4 0.0 slice-done.2
  75.4 5.6 %residual.1 = (bf16[1392,3712]{1,0:T(8,128)(2,1)}, bf16[8,3712]{1,0:T(8,128)(2,1)}) custom-call(bf16[1392,3712]{1,0:T(8,128)(2,1)S(1)} %bitcast.2, bf16[1392,256]{1,0:T(8,128)(2,1)S(1)} %get-tuple-element.6.basis_ref, bf16[2,16,256,128]{3,2,1,0:T(8,128)(2,1)S(1)} %get-tuple-element.7.coef_ref), custom_call_target="tpu_custom_call" | custom-call | flops 2645557248 | bytes 20668416 | tf_op jit(solution)/shard_map/residual/pallas_call | solution.py:491
  (1 shorter events, 0.0 us)
Async XLA Ops:
  0.6 74.7 %slice-start = ((s8[10334208]{0:T(1024)(128)(4,1)}), s8[4194304]{0:T(1024)(128)(4,1)S(1)}, s32[]{:S(2)}) async-start(s8[10334208]{0:T(1024)(128)(4,1)} %bitcast.1), calls=%async_computation | async-start | bytes 8388608
  0.6 74.7 %slice-start.1 = ((s8[10334208]{0:T(1024)(128)(4,1)}), s8[4194304]{0:T(1024)(128)(4,1)S(1)}, s32[]{:S(2)}) async-start(s8[10334208]{0:T(1024)(128)(4,1)} %bitcast.1), calls=%async_computation.1 | async-start | bytes 8388608
  0.7 74.7 %slice-start.2 = ((s8[10334208]{0:T(1024)(128)(4,1)}), s8[1945600]{0:T(1024)(128)(4,1)S(1)}, s32[]{:S(2)}) async-start(s8[10334208]{0:T(1024)(128)(4,1)} %bitcast.1), calls=%async_computation.2 | async-start | bytes 3891200

commit v6 on v5

--- a/solution.py
+++ b/solution.py
@@ -136,7 +136,7 @@
             copy.wait_send()
         pending.clear()
 
-    def gather16(blk, u, v, share, meanwhile):
+    def gather16(blk, u, v, share, meanwhile, early):
         (pu, su), (pv, sv) = u, v
 
         def at_u(step):
@@ -155,6 +155,7 @@
             block = blk(a, pv)
             along_v.append((a, {t: send(block, block, at_v(t)) for t in (2, 1, 3)}))
             shared.append(share(a, pv))
+        early()
         for a, copies in along_v:
             for t in (1, 3, 2):
                 copies[t].wait_recv()
@@ -198,7 +199,7 @@
         load_w.wait()
         part_f[...] = rows_dot(pl.ds(0, PAD), my_off, 0, WIDE)
 
-    gather16(sketch_block, axis1, axis2, share_sketch, own_columns)
+    gather16(sketch_block, axis1, axis2, share_sketch, own_columns, lambda: None)
     mate_only = (1 - core) * WIDE
 
     def piece(step, start, size):
@@ -320,7 +321,7 @@
                 copy.wait_recv()
             gram_y[0] = gram_z[0] + gram_z[1] + gram_z[2] + gram_z[3]
             gram_stage = [send(gram_y.at[0], gram_y.at[t], y_peer(t)) for t in (2, 1, 3)]
-        peers_u = [(t, mod4(p1 + t)) for t in (2, 1, 3)]
+        peers_u = [(t, mod4(p1 + t)) for t in (1, 3, 2)]
         scatter.append([send(z_b.at[j, a1], z_in.at[j, t - 1], chip_peer(a1, p2)) for t, a1 in peers_u])
 
     def row_sum(j):
@@ -402,7 +403,7 @@
         q_high, q_low = split(dot_split(poly[pl.ds(RANK, RANK), :], poly[pl.ds(0, RANK), :]))
         basis_out[...] = (dot(own, q_high) + dot(own, q_low)).astype(BF16)
 
-    gather16(coef_block, axis2, axis1, share_coef, basis_rows)
+    gather16(coef_block, axis2, axis1, share_coef, lambda: None, basis_rows)
     assert count[0] <= COPIES, count[0]
 
 

time: 81.3 us -> 81.3 us (level)
  no operation moved by 1% of the time
where the time goes in v6:
time: 81.3 us; the launch traced here: 81.1 us
  Pallas kernels  80.3 us (99%)
  between operations  0.85 us (1%)
    pallas_call x1, Pallas kernels, shards(): pl.pallas_call(main_kernel, out_shape=(jax.ShapeDtypeStruct((ROWS, RANK),...  74.7 us
    pallas_call x1, Pallas kernels, shards(): pl.pallas_call(residual_kernel, out_shape=(jax.ShapeDtypeStruct((ROWS, CO...  5.59 us

profile of v6, /device:TPU:1, one launch (start us, length us, event | category | flops | bytes accessed | tf_op | source)
XLA Modules:
  0.0 81.1 jit_solution(1045088991819894554)
XLA Ops:
  0.6 0.0 slice-start
  0.6 0.0 slice-start.1
  0.7 0.0 slice-start.2
  0.7 74.7 %polar_basis.1 = (bf16[1392,256]{1,0:T(8,128)(2,1)S(1)}, bf16[2,16,256,128]{3,2,1,0:T(8,128)(2,1)S(1)}) custom-call(bf16[1392,3712]{1,0:T(8,128)(2,1)} %w_ref.1, bf16[8,3712]{1,0:T(8,128)(2,1)} %bitcast.3), custom_call_target="tpu_custom_call" | custom-call | flops 5291114496 | bytes 10334208 | tf_op jit(solution)/shard_map/polar_basis/pallas_call | solution.py:443
  75.4 0.0 slice-done
  75.4 0.0 slice-done.1
  75.4 0.0 slice-done.2
  75.4 5.6 %residual.1 = (bf16[1392,3712]{1,0:T(8,128)(2,1)}, bf16[8,3712]{1,0:T(8,128)(2,1)}) custom-call(bf16[1392,3712]{1,0:T(8,128)(2,1)S(1)} %bitcast.2, bf16[1392,256]{1,0:T(8,128)(2,1)S(1)} %get-tuple-element.6.basis_ref, bf16[2,16,256,128]{3,2,1,0:T(8,128)(2,1)S(1)} %get-tuple-element.7.coef_ref), custom_call_target="tpu_custom_call" | custom-call | flops 2645557248 | bytes 20668416 | tf_op jit(solution)/shard_map/residual/pallas_call | solution.py:492
  (1 shorter events, 0.0 us)
Async XLA Ops:
  0.6 74.7 %slice-start = ((s8[10334208]{0:T(1024)(128)(4,1)}), s8[4194304]{0:T(1024)(128)(4,1)S(1)}, s32[]{:S(2)}) async-start(s8[10334208]{0:T(1024)(128)(4,1)} %bitcast.1), calls=%async_computation | async-start | bytes 8388608
  0.6 74.7 %slice-start.1 = ((s8[10334208]{0:T(1024)(128)(4,1)}), s8[4194304]{0:T(1024)(128)(4,1)S(1)}, s32[]{:S(2)}) async-start(s8[10334208]{0:T(1024)(128)(4,1)} %bitcast.1), calls=%async_computation.1 | async-start | bytes 8388608
  0.7 74.7 %slice-start.2 = ((s8[10334208]{0:T(1024)(128)(4,1)}), s8[1945600]{0:T(1024)(128)(4,1)S(1)}, s32[]{:S(2)}) async-start(s8[10334208]{0:T(1024)(128)(4,1)} %bitcast.1), calls=%async_computation.2 | async-start | bytes 3891200

commit v7 on v6

--- a/solution.py
+++ b/solution.py
@@ -131,10 +131,10 @@
         pending.append(copy)
         return copy
 
-    def drain():
-        for copy in pending:
+    def drain(first=None):
+        for copy in pending[:first]:
             copy.wait_send()
-        pending.clear()
+        del pending[:first]
 
     def gather16(blk, u, v, share, meanwhile, early):
         (pu, su), (pv, sv) = u, v
@@ -145,10 +145,12 @@
         def at_v(step):
             return {"wide": (pu * su + mod4(pv + step) * sv) * 2 + core}
 
+        before = len(pending)
         own = blk(pu, pv)
         along_u = {s: send(own, own, at_u(s)) for s in (2, 1, 3)}
         along_v = [(pu, {s: send(own, own, at_v(s)) for s in (2, 1, 3)})]
         shared = [share(pu, pv)]
+        drain(before)
         for s in (1, 3, 2):
             along_u[s].wait_recv()
             a = mod4(pu + 4 - s)
@@ -163,7 +165,6 @@
         meanwhile()
         for copy in shared:
             copy.wait_recv()
-        drain()
 
     axis1, axis2 = (p1, s1), (p2, s2)
     my_off = core * SKIP
@@ -201,6 +202,7 @@
 
     gather16(sketch_block, axis1, axis2, share_sketch, own_columns, lambda: None)
     mate_only = (1 - core) * WIDE
+    before = len(pending)
 
     def piece(step, start, size):
         return pl.ds(pl.multiple_of(mod4(x + step) * CHUNK + start, 16), size)
@@ -228,6 +230,7 @@
         one[3] = send(part_b.at[piece(3, start, half)], one["in"][3], x_peer(3))
     for start, size in STREAMS:
         add_columns(0, start, size)
+    drain(before)
 
     def inbox(one, n, k):
         return img_in[n, k, pl.ds(0, one["half"]), :].astype(F32)
@@ -403,7 +406,7 @@
         q_high, q_low = split(dot_split(poly[pl.ds(RANK, RANK), :], poly[pl.ds(0, RANK), :]))
         basis_out[...] = (dot(own, q_high) + dot(own, q_low)).astype(BF16)
 
-    gather16(coef_block, axis2, axis1, share_coef, lambda: None, basis_rows)
+    gather16(coef_block, axis2, axis1, share_coef, drain, basis_rows)
     assert count[0] <= COPIES, count[0]
 
 

time: 81.3 us -> 81.1 us (level)
  no operation moved by 1% of the time
where the time goes in v7:
time: 81.1 us; the launch traced here: 81 us
  Pallas kernels  80.1 us (99%)
  between operations  0.85 us (1%)
    pallas_call x1, Pallas kernels, shards(): pl.pallas_call(main_kernel, out_shape=(jax.ShapeDtypeStruct((ROWS, RANK),...  74.5 us
    pallas_call x1, Pallas kernels, shards(): pl.pallas_call(residual_kernel, out_shape=(jax.ShapeDtypeStruct((ROWS, CO...  5.59 us

profile of v7, /device:TPU:1, one launch (start us, length us, event | category | flops | bytes accessed | tf_op | source)
XLA Modules:
  0.0 81.0 jit_solution(6737573690735842361)
XLA Ops:
  0.6 0.0 slice-start
  0.6 0.0 slice-start.1
  0.7 0.0 slice-start.2
  0.7 74.5 %polar_basis.1 = (bf16[1392,256]{1,0:T(8,128)(2,1)S(1)}, bf16[2,16,256,128]{3,2,1,0:T(8,128)(2,1)S(1)}) custom-call(bf16[1392,3712]{1,0:T(8,128)(2,1)} %w_ref.1, bf16[8,3712]{1,0:T(8,128)(2,1)} %bitcast.3), custom_call_target="tpu_custom_call" | custom-call | flops 5291114496 | bytes 10334208 | tf_op jit(solution)/shard_map/polar_basis/pallas_call | solution.py:446
  75.2 0.0 slice-done
  75.2 0.0 slice-done.1
  75.2 0.0 slice-done.2
  75.2 5.6 %residual.1 = (bf16[1392,3712]{1,0:T(8,128)(2,1)}, bf16[8,3712]{1,0:T(8,128)(2,1)}) custom-call(bf16[1392,3712]{1,0:T(8,128)(2,1)S(1)} %bitcast.2, bf16[1392,256]{1,0:T(8,128)(2,1)S(1)} %get-tuple-element.6.basis_ref, bf16[2,16,256,128]{3,2,1,0:T(8,128)(2,1)S(1)} %get-tuple-element.7.coef_ref), custom_call_target="tpu_custom_call" | custom-call | flops 2645557248 | bytes 20668416 | tf_op jit(solution)/shard_map/residual/pallas_call | solution.py:495
  (1 shorter events, 0.0 us)
Async XLA Ops:
  0.6 74.6 %slice-start = ((s8[10334208]{0:T(1024)(128)(4,1)}), s8[4194304]{0:T(1024)(128)(4,1)S(1)}, s32[]{:S(2)}) async-start(s8[10334208]{0:T(1024)(128)(4,1)} %bitcast.1), calls=%async_computation | async-start | bytes 8388608
  0.6 74.6 %slice-start.1 = ((s8[10334208]{0:T(1024)(128)(4,1)}), s8[4194304]{0:T(1024)(128)(4,1)S(1)}, s32[]{:S(2)}) async-start(s8[10334208]{0:T(1024)(128)(4,1)} %bitcast.1), calls=%async_computation.1 | async-start | bytes 8388608
  0.7 74.6 %slice-start.2 = ((s8[10334208]{0:T(1024)(128)(4,1)}), s8[1945600]{0:T(1024)(128)(4,1)S(1)}, s32[]{:S(2)}) async-start(s8[10334208]{0:T(1024)(128)(4,1)} %bitcast.1), calls=%async_computation.2 | async-start | bytes 3891200
